TPU v7x, 128 devices: a whole 4x4x4 slice. The times are simulated.
128 devices in a mesh: tm: 4 (over x_lo, core), lat: 8 (over z, x_hi), lon: 4 (over y).
Axes of the slice: x: 4 (x_hi: 2, x_lo: 2; x = x_hi * 2 + x_lo), y: 4, z: 4, core: 2. Of those that a mesh axis runs over, the one named last changes fastest.
Arguments:
- forcing: float32 [4, 137, 128, 512], P('tm', None, 'lat', 'lon'), may hold values from -6 to 6
- vertical: float32 [13, 137, 137], replicated, may hold values from -0.5 to 0.5
- lat_factor: float32 [8, 8], replicated, may hold values from -2 to 2
- lon_factor: float32 [32, 32], replicated, may hold values from -1 to 1
Outputs:
- increment: float32 [4, 137, 128, 512], P('tm', None, 'lat', 'lon')
- jump: float32 [4, 137, 128, 512], P('tm', None, 'lat', 'lon')
All inputs are finite; a program needn't handle non-finite values.
Results may differ from a plain program's by a relative error of at most 0.0001.
Values sent between devices are 32-bit elements; how exact they have to be, the bound alone decides.
A program may use at most 64 MiB of HBM per device.

v0:
```python
import jax
import jax.numpy as jnp
from jax import lax
from jax.sharding import PartitionSpec as P

LEVELS = 4
BANDS = 13


HIGH = lax.Precision.HIGHEST


def with_halo(shard, sides, width, wrap):
    for axis, dim in sides:
        size, length = (lax.axis_size(axis), shard.shape[dim])
        up = [(i, (i + 1) % size) for i in range(size if wrap else size - 1)]
        down = [(j, i) for i, j in up]
        last = lax.slice_in_dim(shard, length - width, length, axis=dim)
        initial = lax.slice_in_dim(shard, 0, width, axis=dim)
        before = lax.ppermute(last, axis, up)
        after = lax.ppermute(initial, axis, down)
        shard = jnp.concatenate([before, shard, after], axis=dim)
    return shard


def shifted(block, axis, distance):
    devices = range(lax.axis_size(axis))
    route = [(i - distance, i) for i in devices if i - distance in devices]
    return lax.ppermute(block, axis, route)


def cut(field, start, stop, axis, stride=1):
    return lax.slice_in_dim(field, start, stop, stride, axis)


def analyse(padded, axis):
    half = (padded.shape[axis] - 4) // 2
    even = cut(padded, 0, 2 * half + 3, axis, 2)
    odd = cut(padded, 1, 2 * half + 4, axis, 2)
    detail_ext = cut(odd, 0, half + 1, axis) - 0.5 * (
        cut(even, 0, half + 1, axis) + cut(even, 1, half + 2, axis)
    )
    smooth = cut(even, 1, half + 1, axis) + 0.25 * (
        cut(detail_ext, 0, half, axis) + cut(detail_ext, 1, half + 1, axis)
    )
    return (smooth, cut(detail_ext, 1, half + 1, axis))


def synthesise(smooth_pad, detail_pad, axis):
    half = smooth_pad.shape[axis] - 2
    even = cut(smooth_pad, 1, half + 2, axis) - 0.25 * (
        cut(detail_pad, 0, half + 1, axis) + cut(detail_pad, 1, half + 2, axis)
    )
    odd = cut(detail_pad, 1, half + 1, axis) + 0.5 * (
        cut(even, 0, half, axis) + cut(even, 1, half + 1, axis)
    )
    both = jnp.stack([cut(even, 0, half, axis), odd], axis=axis + 1)
    return both.reshape(odd.shape[:axis] + (2 * half,) + odd.shape[axis + 1 :])


def coarse_band(smooth, lat_factor, lon_factor):
    levels, rows, columns = smooth.shape
    lat_rows = lax.dynamic_slice_in_dim(lat_factor, lax.axis_index("lat") * rows, rows, 0)
    lon_rows = lax.dynamic_slice_in_dim(lon_factor, lax.axis_index("lon") * columns, columns, 0)
    tiles = lax.all_gather(smooth[None], ("lat", "lon"), axis=0, tiled=True)
    lat_count = lax.axis_size("lat")
    lon_count = lax.axis_size("lon")
    whole = tiles.reshape(lat_count, lon_count, levels, rows, columns)
    whole = whole.transpose(2, 0, 3, 1, 4).reshape(levels, lat_count * rows, lon_count * columns)
    mixed = jnp.einsum("ab,kbc->kac", lat_rows, whole, precision=HIGH)
    return jnp.einsum("kac,dc->kad", mixed, lon_rows, precision=HIGH)


def covary(field, vertical, lat_factor, lon_factor):
    smooth = field
    bands = []
    for level in range(LEVELS):
        padded = with_halo(smooth, (("lon", 2),), 2, True)
        lon_s, lon_d = analyse(padded, 2)
        pair = with_halo(jnp.stack([lon_s, lon_d]), (("lat", 2),), 2, False)
        lat_s, lat_d = analyse(pair, 2)
        smooth = lat_s[0]
        details = jnp.stack([lat_s[1], lat_d[0], lat_d[1]])
        bands.append(
            jnp.einsum(
                "bij,bjxy->bixy", vertical[3 * level : 3 * level + 3], details, precision=HIGH
            )
        )
    mixed = coarse_band(smooth, lat_factor, lon_factor)
    smooth = jnp.einsum("ij,jac->iac", vertical[BANDS - 1], mixed, precision=HIGH)
    for level in range(LEVELS - 1, -1, -1):
        band = bands[level]
        quartet = jnp.stack([jnp.stack([smooth, band[0]]), jnp.stack([band[1], band[2]])])
        quartet = with_halo(quartet, (("lat", 3),), 1, False)
        lifted = synthesise(quartet[0], quartet[1], 2)
        lifted = with_halo(lifted, (("lon", 3),), 1, True)
        smooth = synthesise(lifted[0], lifted[1], 2)
    return smooth


def body(forcing, vertical, lat_factor, lon_factor):
    increment = covary(forcing[0], vertical, lat_factor, lon_factor)[None]
    earlier = shifted(increment, "tm", 1)
    return (increment, increment - earlier)


def solution(mesh):
    placed = (P("tm", None, "lat", "lon"), P(), P(), P())
    return jax.shard_map(
        body,
        mesh=mesh,
        in_specs=placed,
        out_specs=(P("tm", None, "lat", "lon"), P("tm", None, "lat", "lon")),
        check_vma=False,
    )
```

profile of v0, /device:TPU:2, one launch (start us, length us, event | category | flops | bytes accessed | tf_op | source)
XLA Modules:
  0.0 285.2 jit_solution(2840824614068962225)
XLA Ops:
  0.6 1.8 copy.28
  2.5 1.6 collective-permute-start
  4.1 1.7 collective-permute-start.1
  5.8 1.9 collective-permute-done
  8.0 1.8 pad_maximum_fusion.3
  10.5 2.9 %slice.583 = f32[137,16,66]{0,2,1:T(8,128)} slice(f32[137,16,132]{0,2,1:T(8,128)S(1)} %pad_maximum_fusion.3), slice={[0:137:1], [0:16:1], [1:132:2]} | slice | bytes 1157376 | tf_op jit(solution)/shard_map/slice | solution.py:33
  15.3 4.0 %collective-permute-start.2 = (f32[2,137,2,64]{1,3,2,0:T(8,128)S(1)}, f32[2,137,2,64]{1,3,2,0:T(8,128)S(1)}, u32[]{:S(2)}, u32[]{:S(2)}) collective-permute-start(f32[2,137,2,64]{1,3,2,0:T(8,128)S(1)} %get-tuple-element.16), channel_id=1, source_target_pairs={{0,4},{4,8},{8,12},{12,16},{16,20},{20,24},{24,28},{1,5},{5,9},{9,... | collective-permute-start | bytes 420872 | tf_op jit(solution)/shard_map/ppermute | solution.py:20
  20.6 2.8 collective-permute-done.2
  23.4 8.8 %collective-permute-done.3 = f32[2,137,2,64]{1,3,2,0:T(8,128)S(1)} collective-permute-done((f32[2,137,2,64]{1,3,2,0:T(8,128)S(1)}, f32[2,137,2,64]{1,3,2,0:T(8,128)S(1)}, u32[]{:S(2)}, u32[]{:S(2)}) %collective-permute-start.3) | collective-permute-done | bytes 140320 | tf_op jit(solution)/shard_map/ppermute | solution.py:21
  34.3 1.8 collective-permute-start.4
  36.0 1.5 collective-permute-start.5
  37.6 1.7 collective-permute-done.4
  41.0 4.0 %collective-permute-start.6 = (f32[2,137,2,32]{1,3,2,0:T(8,128)S(1)}, f32[2,137,2,32]{1,3,2,0:T(8,128)S(1)}, u32[]{:S(2)}, u32[]{:S(2)}) collective-permute-start(f32[2,137,2,32]{1,3,2,0:T(8,128)S(1)} %get-tuple-element.40), channel_id=1, source_target_pairs={{0,4},{4,8},{8,12},{12,16},{16,20},{20,24},{24,28},{1,5},{5,9},{9,... | collective-permute-start | bytes 210440 | tf_op jit(solution)/shard_map/ppermute | solution.py:20
  47.5 5.9 %collective-permute-done.7 = f32[2,137,2,32]{1,3,2,0:T(8,128)S(1)} collective-permute-done((f32[2,137,2,32]{1,3,2,0:T(8,128)S(1)}, f32[2,137,2,32]{1,3,2,0:T(8,128)S(1)}, u32[]{:S(2)}, u32[]{:S(2)}) %collective-permute-start.7) | collective-permute-done | bytes 70176 | tf_op jit(solution)/shard_map/ppermute | solution.py:21
  53.7 1.5 collective-permute-start.8
  55.2 1.8 collective-permute-start.9
  57.0 1.6 collective-permute-done.8
  59.0 5.7 %collective-permute-start.10 = (f32[2,137,2,16]{1,3,2,0:T(8,128)S(1)}, f32[2,137,2,16]{1,3,2,0:T(8,128)S(1)}, u32[]{:S(2)}, u32[]{:S(2)}) collective-permute-start(f32[2,137,2,16]{1,3,2,0:T(8,128)S(1)} %get-tuple-element.64), channel_id=1, source_target_pairs={{0,4},{4,8},{8,12},{12,16},{16,20},{20,24},{24,28},{1,5},{5,9},{9,... | collective-permute-start | bytes 105224 | tf_op jit(solution)/shard_map/ppermute | solution.py:20
  66.6 5.8 %collective-permute-done.11 = f32[2,137,2,16]{1,3,2,0:T(8,128)S(1)} collective-permute-done((f32[2,137,2,16]{1,3,2,0:T(8,128)S(1)}, f32[2,137,2,16]{1,3,2,0:T(8,128)S(1)}, u32[]{:S(2)}, u32[]{:S(2)}) %collective-permute-start.11) | collective-permute-done | bytes 35104 | tf_op jit(solution)/shard_map/ppermute | solution.py:21
  73.9 2.0 collective-permute-start.13
  75.8 1.6 collective-permute-done.12
  78.9 6.1 %collective-permute-start.14 = (f32[2,137,2,8]{1,3,0,2:T(8,128)S(1)}, f32[2,137,2,8]{1,3,0,2:T(8,128)S(1)}, u32[]{:S(2)}, u32[]{:S(2)}) collective-permute-start(f32[2,137,2,8]{1,3,0,2:T(8,128)S(1)} %pad_maximum_fusion.32), channel_id=1, source_target_pairs={{0,4},{4,8},{8,12},{12,16},{16,20},{20,24},{24,28},{1,5},{5,9},{9,... | collective-permute-start | bytes 52616 | tf_op jit(solution)/shard_map/ppermute | solution.py:20
  85.0 1.6 collective-permute-done.14
  87.1 92.8 %all_gather.3 = f32[32,137,1,8]{1,3,2,0:T(8,128)S(1)} all-gather(f32[1,137,1,8]{1,3,2,0:T(8,128)S(1)} %get-tuple-element.99), channel_id=1, replica_groups=mesh['tm'=4,'lat'=8,'lon'=4] {'lat','lon'}, dimensions={0}, use_global_device_ids=true | all-gather | bytes 144672 | tf_op jit(solution)/shard_map/all_gather | solution.py:65
  183.0 6.1 %collective-permute-start.16 = (f32[2,2,137,1,8]{2,4,1,3,0:T(8,128)S(1)}, f32[2,2,137,1,8]{2,4,1,3,0:T(8,128)S(1)}, u32[]{:S(2)}, u32[]{:S(2)}) collective-permute-start(f32[2,2,137,1,8]{2,4,1,3,0:T(8,128)S(1)} %pad_maximum_fusion.33), channel_id=1, source_target_pairs={{0,4},{4,8},{8,12},{12,16},{16,20},{20,24},{24,28},{1,5},{5,9},{9,... | collective-permute-start | bytes 52616 | tf_op jit(solution)/shard_map/ppermute | solution.py:20
  190.8 3.2 %collective-permute-start.19 = (f32[2,137,2,1]{1,3,0,2:T(1,128)S(1)}, f32[2,137,2,1]{1,3,0,2:T(1,128)S(1)}, u32[]{:S(2)}, u32[]{:S(2)}) collective-permute-start(f32[2,137,2,1]{1,3,0,2:T(1,128)S(1)} %get-tuple-element.87), channel_id=1, source_target_pairs={{1,0},{2,1},{3,2},{0,3},{5,4},{6,5},{7,6},{4,7},{9,8},{10,9},{11,1... | collective-permute-start | bytes 6584 | tf_op jit(solution)/shard_map/ppermute | solution.py:21
  194.1 1.6 collective-permute-done.18
  195.8 5.7 %collective-permute-start.20 = (f32[2,2,137,1,16]{2,4,3,1,0:T(8,128)S(1)}, f32[2,2,137,1,16]{2,4,3,1,0:T(8,128)S(1)}, u32[]{:S(2)}, u32[]{:S(2)}) collective-permute-start(f32[2,2,137,1,16]{2,4,3,1,0:T(8,128)S(1)} %get-tuple-element.62), channel_id=1, source_target_pairs={{0,4},{4,8},{8,12},{12,16},{16,20},{20,24},{24,28},{1,5},{5,9},{9,... | collective-permute-start | bytes 105224 | tf_op jit(solution)/shard_map/ppermute | solution.py:20
  203.4 5.8 %collective-permute-done.21 = f32[2,2,137,1,16]{2,4,3,1,0:T(8,128)S(1)} collective-permute-done((f32[2,2,137,1,16]{2,4,3,1,0:T(8,128)S(1)}, f32[2,2,137,1,16]{2,4,3,1,0:T(8,128)S(1)}, u32[]{:S(2)}, u32[]{:S(2)}) %collective-permute-start.21) | collective-permute-done | bytes 35104 | tf_op jit(solution)/shard_map/ppermute | solution.py:21
  209.5 3.4 %collective-permute-start.23 = (f32[2,137,4,1]{1,3,2,0:T(1,128)S(1)}, f32[2,137,4,1]{1,3,2,0:T(1,128)S(1)}, u32[]{:S(2)}, u32[]{:S(2)}) collective-permute-start(f32[2,137,4,1]{1,3,2,0:T(1,128)S(1)} %get-tuple-element.61), channel_id=1, source_target_pairs={{1,0},{2,1},{3,2},{0,3},{5,4},{6,5},{7,6},{4,7},{9,8},{10,9},{11,1... | collective-permute-start | bytes 13160 | tf_op jit(solution)/shard_map/ppermute | solution.py:21
  212.9 1.5 collective-permute-done.22
  215.8 4.3 %collective-permute-start.24 = (f32[2,2,137,1,32]{2,4,3,1,0:T(8,128)S(1)}, f32[2,2,137,1,32]{2,4,3,1,0:T(8,128)S(1)}, u32[]{:S(2)}, u32[]{:S(2)}) collective-permute-start(f32[2,2,137,1,32]{2,4,3,1,0:T(8,128)S(1)} %get-tuple-element.38), channel_id=1, source_target_pairs={{0,4},{4,8},{8,12},{12,16},{16,20},{20,24},{24,28},{1,5},{5,9},{9,... | collective-permute-start | bytes 210440 | tf_op jit(solution)/shard_map/ppermute | solution.py:20
  220.0 1.5 collective-permute-start.25
  221.5 2.5 fusion.4
  224.1 4.3 %collective-permute-done.25 = f32[2,2,137,1,32]{2,4,3,1,0:T(8,128)S(1)} collective-permute-done((f32[2,2,137,1,32]{2,4,3,1,0:T(8,128)S(1)}, f32[2,2,137,1,32]{2,4,3,1,0:T(8,128)S(1)}, u32[]{:S(2)}, u32[]{:S(2)}) %collective-permute-start.25) | collective-permute-done | bytes 70176 | tf_op jit(solution)/shard_map/ppermute | solution.py:21
  228.8 1.5 collective-permute-start.26
  230.3 2.0 collective-permute-start.27
  232.3 1.5 collective-permute-done.26
  235.5 2.8 collective-permute-start.28
  239.6 2.6 collective-permute-done.28
  242.2 5.9 %collective-permute-done.29 = f32[2,2,137,1,64]{2,4,3,1,0:T(8,128)S(1)} collective-permute-done((f32[2,2,137,1,64]{2,4,3,1,0:T(8,128)S(1)}, f32[2,2,137,1,64]{2,4,3,1,0:T(8,128)S(1)}, u32[]{:S(2)}, u32[]{:S(2)}) %collective-permute-start.29) | collective-permute-done | bytes 140320 | tf_op jit(solution)/shard_map/ppermute | solution.py:21
  249.7 2.1 collective-permute-start.30
  253.0 1.9 collective-permute-done.30
  259.2 1.9 collective-permute-start.32
  261.1 15.1 %collective-permute-done.32 = f32[1,137,16,128]{3,2,1,0:T(8,128)} collective-permute-done((f32[1,137,16,128]{3,2,1,0:T(8,128)S(1)}, f32[1,137,16,128]{3,2,1,0:T(8,128)}, u32[]{:S(2)}, u32[]{:S(2)}) %collective-permute-start.32) | collective-permute-done | bytes 1122336 | tf_op jit(solution)/shard_map/ppermute | solution.py:29
  276.2 3.0 %copy.43 = f32[1,137,16,128]{1,2,3,0:T(8,128)} copy(f32[1,137,16,128]{3,2,1,0:T(8,128)} %collective-permute-done.32) | data formatting | bytes 2244608 | tf_op jit(solution)/shard_map/ppermute | solution.py:29
  279.2 3.2 %bitcast_subtract_fusion = f32[1,137,16,128]{1,2,3,0:T(8,128)} fusion(f32[1,137,16,128]{1,2,3,0:T(8,128)} %copy.43, f32[137,16,64,2]{0,1,3,2:T(8,128)S(1)} %copy.41), kind=kLoop, calls=%fused_computation.233 | loop fusion | flops 280576 | bytes 3366912 | tf_op jit(solution)/shard_map/sub | solution.py:104
  282.4 2.8 copy.45
  (168 shorter events, 34.6 us)
Async XLA Ops:
  0.6 180.6 %copy-start = (f32[32,32]{1,0:T(8,128)S(1)}, f32[32,32]{1,0:T(8,128)}, u32[]{:S(2)}) copy-start(f32[32,32]{1,0:T(8,128)} %param.7) | copy-start | bytes 12292
  2.4 5.2 %copy-start.2 = (f32[1,137,16,128]{1,3,2,0:T(8,128)}, f32[1,137,16,128]{1,3,2,0:T(8,128)S(1)}, u32[]{:S(2)}) copy-start(f32[1,137,16,128]{1,3,2,0:T(8,128)S(1)} %copy.28) | copy-start | bytes 3366916
  2.5 5.2 %collective-permute-start = (f32[137,16,2]{0,2,1:T(2,128)S(1)}, f32[137,16,2]{0,2,1:T(2,128)S(1)}, u32[]{:S(2)}, u32[]{:S(2)}) collective-permute-start(f32[137,16,2]{0,2,1:T(2,128)S(1)} %get-tuple-element.18), channel_id=1, source_target_pairs={{0,1},{1,2},{2,3},{3,0},{4,5},{5,6},{6,7},{7,4},{8,9},{9,10},{10,1... | collective-permute-start | bytes 52616 | tf_op jit(solution)/shard_map/ppermute | solution.py:20
  4.1 3.9 %collective-permute-start.1 = (f32[137,16,2]{0,2,1:T(2,128)S(1)}, f32[137,16,2]{0,2,1:T(2,128)S(1)}, u32[]{:S(2)}, u32[]{:S(2)}) collective-permute-start(f32[137,16,2]{0,2,1:T(2,128)S(1)} %get-tuple-element.19), channel_id=1, source_target_pairs={{1,0},{2,1},{3,2},{0,3},{5,4},{6,5},{7,6},{4,7},{9,8},{10,9},{11,1... | collective-permute-start | bytes 52616 | tf_op jit(solution)/shard_map/ppermute | solution.py:21
  15.3 8.2 %collective-permute-start.2 = (f32[2,137,2,64]{1,3,2,0:T(8,128)S(1)}, f32[2,137,2,64]{1,3,2,0:T(8,128)S(1)}, u32[]{:S(2)}, u32[]{:S(2)}) collective-permute-start(f32[2,137,2,64]{1,3,2,0:T(8,128)S(1)} %get-tuple-element.16), channel_id=1, source_target_pairs={{0,4},{4,8},{8,12},{12,16},{16,20},{20,24},{24,28},{1,5},{5,9},{9,... | collective-permute-start | bytes 420872 | tf_op jit(solution)/shard_map/ppermute | solution.py:20
  19.3 12.9 %collective-permute-start.3 = (f32[2,137,2,64]{1,3,2,0:T(8,128)S(1)}, f32[2,137,2,64]{1,3,2,0:T(8,128)S(1)}, u32[]{:S(2)}, u32[]{:S(2)}) collective-permute-start(f32[2,137,2,64]{1,3,2,0:T(8,128)S(1)} %get-tuple-element.17), channel_id=1, source_target_pairs={{4,0},{8,4},{12,8},{16,12},{20,16},{24,20},{28,24},{5,1},{9,5},{13... | collective-permute-start | bytes 420872 | tf_op jit(solution)/shard_map/ppermute | solution.py:21
  34.3 5.0 %collective-permute-start.4 = (f32[137,8,2]{0,2,1:T(2,128)S(1)}, f32[137,8,2]{0,2,1:T(2,128)S(1)}, u32[]{:S(2)}, u32[]{:S(2)}) collective-permute-start(f32[137,8,2]{0,2,1:T(2,128)S(1)} %get-tuple-element.42), channel_id=1, source_target_pairs={{0,1},{1,2},{2,3},{3,0},{4,5},{5,6},{6,7},{7,4},{8,9},{9,10},{10,1... | collective-permute-start | bytes 26312 | tf_op jit(solution)/shard_map/ppermute | solution.py:20
  36.0 3.7 %collective-permute-start.5 = (f32[137,8,2]{0,2,1:T(2,128)S(1)}, f32[137,8,2]{0,2,1:T(2,128)S(1)}, u32[]{:S(2)}, u32[]{:S(2)}) collective-permute-start(f32[137,8,2]{0,2,1:T(2,128)S(1)} %get-tuple-element.43), channel_id=1, source_target_pairs={{1,0},{2,1},{3,2},{0,3},{5,4},{6,5},{7,6},{4,7},{9,8},{10,9},{11,1... | collective-permute-start | bytes 26312 | tf_op jit(solution)/shard_map/ppermute | solution.py:21
  41.0 6.5 %collective-permute-start.6 = (f32[2,137,2,32]{1,3,2,0:T(8,128)S(1)}, f32[2,137,2,32]{1,3,2,0:T(8,128)S(1)}, u32[]{:S(2)}, u32[]{:S(2)}) collective-permute-start(f32[2,137,2,32]{1,3,2,0:T(8,128)S(1)} %get-tuple-element.40), channel_id=1, source_target_pairs={{0,4},{4,8},{8,12},{12,16},{16,20},{20,24},{24,28},{1,5},{5,9},{9,... | collective-permute-start | bytes 210440 | tf_op jit(solution)/shard_map/ppermute | solution.py:20
  45.0 8.4 %collective-permute-start.7 = (f32[2,137,2,32]{1,3,2,0:T(8,128)S(1)}, f32[2,137,2,32]{1,3,2,0:T(8,128)S(1)}, u32[]{:S(2)}, u32[]{:S(2)}) collective-permute-start(f32[2,137,2,32]{1,3,2,0:T(8,128)S(1)} %get-tuple-element.41), channel_id=1, source_target_pairs={{4,0},{8,4},{12,8},{16,12},{20,16},{24,20},{28,24},{5,1},{9,5},{13... | collective-permute-start | bytes 210440 | tf_op jit(solution)/shard_map/ppermute | solution.py:21
  53.7 4.9 %collective-permute-start.8 = (f32[137,4,2]{0,2,1:T(2,128)S(1)}, f32[137,4,2]{0,2,1:T(2,128)S(1)}, u32[]{:S(2)}, u32[]{:S(2)}) collective-permute-start(f32[137,4,2]{0,2,1:T(2,128)S(1)} %get-tuple-element.66), channel_id=1, source_target_pairs={{0,1},{1,2},{2,3},{3,0},{4,5},{5,6},{6,7},{7,4},{8,9},{9,10},{10,1... | collective-permute-start | bytes 13160 | tf_op jit(solution)/shard_map/ppermute | solution.py:20
  55.2 3.7 %collective-permute-start.9 = (f32[137,4,2]{0,2,1:T(2,128)S(1)}, f32[137,4,2]{0,2,1:T(2,128)S(1)}, u32[]{:S(2)}, u32[]{:S(2)}) collective-permute-start(f32[137,4,2]{0,2,1:T(2,128)S(1)} %get-tuple-element.67), channel_id=1, source_target_pairs={{1,0},{2,1},{3,2},{0,3},{5,4},{6,5},{7,6},{4,7},{9,8},{10,9},{11,1... | collective-permute-start | bytes 13160 | tf_op jit(solution)/shard_map/ppermute | solution.py:21
  59.0 27.6 %copy-start.5 = (f32[13,137,137]{2,1,0:T(8,128)S(1)}, f32[13,137,137]{2,1,0:T(8,128)}, u32[]{:S(2)}) copy-start(f32[13,137,137]{2,1,0:T(8,128)} %param.5) | copy-start | bytes 2927968
  59.0 7.6 %collective-permute-start.10 = (f32[2,137,2,16]{1,3,2,0:T(8,128)S(1)}, f32[2,137,2,16]{1,3,2,0:T(8,128)S(1)}, u32[]{:S(2)}, u32[]{:S(2)}) collective-permute-start(f32[2,137,2,16]{1,3,2,0:T(8,128)S(1)} %get-tuple-element.64), channel_id=1, source_target_pairs={{0,4},{4,8},{8,12},{12,16},{16,20},{20,24},{24,28},{1,5},{5,9},{9,... | collective-permute-start | bytes 105224 | tf_op jit(solution)/shard_map/ppermute | solution.py:20
  64.7 7.7 %collective-permute-start.11 = (f32[2,137,2,16]{1,3,2,0:T(8,128)S(1)}, f32[2,137,2,16]{1,3,2,0:T(8,128)S(1)}, u32[]{:S(2)}, u32[]{:S(2)}) collective-permute-start(f32[2,137,2,16]{1,3,2,0:T(8,128)S(1)} %get-tuple-element.65), channel_id=1, source_target_pairs={{4,0},{8,4},{12,8},{16,12},{20,16},{24,20},{28,24},{5,1},{9,5},{13... | collective-permute-start | bytes 105224 | tf_op jit(solution)/shard_map/ppermute | solution.py:21
  72.5 4.9 %collective-permute-start.12 = (f32[137,2,2]{0,2,1:T(2,128)S(1)}, f32[137,2,2]{0,2,1:T(2,128)S(1)}, u32[]{:S(2)}, u32[]{:S(2)}) collective-permute-start(f32[137,2,2]{0,2,1:T(2,128)S(1)} %get-tuple-element.94), channel_id=1, source_target_pairs={{0,1},{1,2},{2,3},{3,0},{4,5},{5,6},{6,7},{7,4},{8,9},{9,10},{10,1... | collective-permute-start | bytes 6584 | tf_op jit(solution)/shard_map/ppermute | solution.py:20
  73.9 3.6 %collective-permute-start.13 = (f32[137,2,2]{0,2,1:T(2,128)S(1)}, f32[137,2,2]{0,2,1:T(2,128)S(1)}, u32[]{:S(2)}, u32[]{:S(2)}) collective-permute-start(f32[137,2,2]{0,2,1:T(2,128)S(1)} %get-tuple-element.95), channel_id=1, source_target_pairs={{1,0},{2,1},{3,2},{0,3},{5,4},{6,5},{7,6},{4,7},{9,8},{10,9},{11,1... | collective-permute-start | bytes 6584 | tf_op jit(solution)/shard_map/ppermute | solution.py:21
  77.6 7.4 %collective-permute-start.15 = (f32[2,137,2,8]{1,3,0,2:T(8,128)S(1)}, f32[2,137,2,8]{1,3,0,2:T(8,128)S(1)}, u32[]{:S(2)}, u32[]{:S(2)}) collective-permute-start(f32[2,137,2,8]{1,3,0,2:T(8,128)S(1)} %pad_maximum_fusion.32), channel_id=1, source_target_pairs={{4,0},{8,4},{12,8},{16,12},{20,16},{24,20},{28,24},{5,1},{9,5},{13... | collective-permute-start | bytes 52616 | tf_op jit(solution)/shard_map/ppermute | solution.py:21
  78.9 7.6 %collective-permute-start.14 = (f32[2,137,2,8]{1,3,0,2:T(8,128)S(1)}, f32[2,137,2,8]{1,3,0,2:T(8,128)S(1)}, u32[]{:S(2)}, u32[]{:S(2)}) collective-permute-start(f32[2,137,2,8]{1,3,0,2:T(8,128)S(1)} %pad_maximum_fusion.32), channel_id=1, source_target_pairs={{0,4},{4,8},{8,12},{12,16},{16,20},{20,24},{24,28},{1,5},{5,9},{9,... | collective-permute-start | bytes 52616 | tf_op jit(solution)/shard_map/ppermute | solution.py:20
  181.7 7.9 %collective-permute-start.17 = (f32[2,2,137,1,8]{2,4,1,3,0:T(8,128)S(1)}, f32[2,2,137,1,8]{2,4,1,3,0:T(8,128)S(1)}, u32[]{:S(2)}, u32[]{:S(2)}) collective-permute-start(f32[2,2,137,1,8]{2,4,1,3,0:T(8,128)S(1)} %pad_maximum_fusion.33), channel_id=1, source_target_pairs={{4,0},{8,4},{12,8},{16,12},{20,16},{24,20},{28,24},{5,1},{9,5},{13... | collective-permute-start | bytes 52616 | tf_op jit(solution)/shard_map/ppermute | solution.py:21
  183.0 7.6 %collective-permute-start.16 = (f32[2,2,137,1,8]{2,4,1,3,0:T(8,128)S(1)}, f32[2,2,137,1,8]{2,4,1,3,0:T(8,128)S(1)}, u32[]{:S(2)}, u32[]{:S(2)}) collective-permute-start(f32[2,2,137,1,8]{2,4,1,3,0:T(8,128)S(1)} %pad_maximum_fusion.33), channel_id=1, source_target_pairs={{0,4},{4,8},{8,12},{12,16},{16,20},{20,24},{24,28},{1,5},{5,9},{9,... | collective-permute-start | bytes 52616 | tf_op jit(solution)/shard_map/ppermute | solution.py:20
  190.8 4.9 %collective-permute-start.18 = (f32[2,137,2,1]{1,3,0,2:T(1,128)S(1)}, f32[2,137,2,1]{1,3,0,2:T(1,128)S(1)}, u32[]{:S(2)}, u32[]{:S(2)}) collective-permute-start(f32[2,137,2,1]{1,3,0,2:T(1,128)S(1)} %get-tuple-element.86), channel_id=1, source_target_pairs={{0,1},{1,2},{2,3},{3,0},{4,5},{5,6},{6,7},{7,4},{8,9},{9,10},{10,1... | collective-permute-start | bytes 6584 | tf_op jit(solution)/shard_map/ppermute | solution.py:20
  190.8 4.8 %collective-permute-start.19 = (f32[2,137,2,1]{1,3,0,2:T(1,128)S(1)}, f32[2,137,2,1]{1,3,0,2:T(1,128)S(1)}, u32[]{:S(2)}, u32[]{:S(2)}) collective-permute-start(f32[2,137,2,1]{1,3,0,2:T(1,128)S(1)} %get-tuple-element.87), channel_id=1, source_target_pairs={{1,0},{2,1},{3,2},{0,3},{5,4},{6,5},{7,6},{4,7},{9,8},{10,9},{11,1... | collective-permute-start | bytes 6584 | tf_op jit(solution)/shard_map/ppermute | solution.py:21
  195.8 7.6 %collective-permute-start.20 = (f32[2,2,137,1,16]{2,4,3,1,0:T(8,128)S(1)}, f32[2,2,137,1,16]{2,4,3,1,0:T(8,128)S(1)}, u32[]{:S(2)}, u32[]{:S(2)}) collective-permute-start(f32[2,2,137,1,16]{2,4,3,1,0:T(8,128)S(1)} %get-tuple-element.62), channel_id=1, source_target_pairs={{0,4},{4,8},{8,12},{12,16},{16,20},{20,24},{24,28},{1,5},{5,9},{9,... | collective-permute-start | bytes 105224 | tf_op jit(solution)/shard_map/ppermute | solution.py:20
  201.5 7.7 %collective-permute-start.21 = (f32[2,2,137,1,16]{2,4,3,1,0:T(8,128)S(1)}, f32[2,2,137,1,16]{2,4,3,1,0:T(8,128)S(1)}, u32[]{:S(2)}, u32[]{:S(2)}) collective-permute-start(f32[2,2,137,1,16]{2,4,3,1,0:T(8,128)S(1)} %get-tuple-element.63), channel_id=1, source_target_pairs={{4,0},{8,4},{12,8},{16,12},{20,16},{24,20},{28,24},{5,1},{9,5},{13... | collective-permute-start | bytes 105224 | tf_op jit(solution)/shard_map/ppermute | solution.py:21
  203.4 11.1 %copy-start.6 = (f32[3,137,4,32]{1,3,2,0:T(8,128)}, f32[3,137,4,32]{1,3,2,0:T(8,128)S(1)}, u32[]{:S(2)}) copy-start(f32[3,137,4,32]{1,3,2,0:T(8,128)S(1)} %convolution_bitcast_fusion) | copy-start | bytes 631300
  209.4 5.1 %collective-permute-start.22 = (f32[2,137,4,1]{1,3,2,0:T(1,128)S(1)}, f32[2,137,4,1]{1,3,2,0:T(1,128)S(1)}, u32[]{:S(2)}, u32[]{:S(2)}) collective-permute-start(f32[2,137,4,1]{1,3,2,0:T(1,128)S(1)} %get-tuple-element.60), channel_id=1, source_target_pairs={{0,1},{1,2},{2,3},{3,0},{4,5},{5,6},{6,7},{7,4},{8,9},{9,10},{10,1... | collective-permute-start | bytes 13160 | tf_op jit(solution)/shard_map/ppermute | solution.py:20
  209.5 5.0 %collective-permute-start.23 = (f32[2,137,4,1]{1,3,2,0:T(1,128)S(1)}, f32[2,137,4,1]{1,3,2,0:T(1,128)S(1)}, u32[]{:S(2)}, u32[]{:S(2)}) collective-permute-start(f32[2,137,4,1]{1,3,2,0:T(1,128)S(1)} %get-tuple-element.61), channel_id=1, source_target_pairs={{1,0},{2,1},{3,2},{0,3},{5,4},{6,5},{7,6},{4,7},{9,8},{10,9},{11,1... | collective-permute-start | bytes 13160 | tf_op jit(solution)/shard_map/ppermute | solution.py:21
  214.5 7.0 %copy-start.4 = (f32[2,137,8,64]{1,3,2,0:T(8,128)S(1)}, f32[2,137,8,64]{1,3,2,0:T(8,128)}, u32[]{:S(2)}) copy-start(f32[2,137,8,64]{1,3,2,0:T(8,128)} %get-tuple-element.25) | copy-start | bytes 1683460
  214.5 1.2 slice-start.1
  215.8 8.3 %collective-permute-start.24 = (f32[2,2,137,1,32]{2,4,3,1,0:T(8,128)S(1)}, f32[2,2,137,1,32]{2,4,3,1,0:T(8,128)S(1)}, u32[]{:S(2)}, u32[]{:S(2)}) collective-permute-start(f32[2,2,137,1,32]{2,4,3,1,0:T(8,128)S(1)} %get-tuple-element.38), channel_id=1, source_target_pairs={{0,4},{4,8},{8,12},{12,16},{16,20},{20,24},{24,28},{1,5},{5,9},{9,... | collective-permute-start | bytes 210440 | tf_op jit(solution)/shard_map/ppermute | solution.py:20
  220.0 8.4 %collective-permute-start.25 = (f32[2,2,137,1,32]{2,4,3,1,0:T(8,128)S(1)}, f32[2,2,137,1,32]{2,4,3,1,0:T(8,128)S(1)}, u32[]{:S(2)}, u32[]{:S(2)}) collective-permute-start(f32[2,2,137,1,32]{2,4,3,1,0:T(8,128)S(1)} %get-tuple-element.39), channel_id=1, source_target_pairs={{4,0},{8,4},{12,8},{16,12},{20,16},{24,20},{28,24},{5,1},{9,5},{13... | collective-permute-start | bytes 210440 | tf_op jit(solution)/shard_map/ppermute | solution.py:21
  224.0 8.3 %copy-start.3 = (f32[3,137,8,64]{1,3,2,0:T(8,128)}, f32[3,137,8,64]{1,3,2,0:T(8,128)S(1)}, u32[]{:S(2)}) copy-start(f32[3,137,8,64]{1,3,2,0:T(8,128)S(1)} %fusion.4) | copy-start | bytes 2525188
  228.8 5.1 %collective-permute-start.26 = (f32[2,137,8,1]{1,3,2,0:T(1,128)S(1)}, f32[2,137,8,1]{1,3,2,0:T(1,128)S(1)}, u32[]{:S(2)}, u32[]{:S(2)}) collective-permute-start(f32[2,137,8,1]{1,3,2,0:T(1,128)S(1)} %get-tuple-element.36), channel_id=1, source_target_pairs={{0,1},{1,2},{2,3},{3,0},{4,5},{5,6},{6,7},{7,4},{8,9},{9,10},{10,1... | collective-permute-start | bytes 26312 | tf_op jit(solution)/shard_map/ppermute | solution.py:20
  230.3 3.7 %collective-permute-start.27 = (f32[2,137,8,1]{1,3,2,0:T(1,128)S(1)}, f32[2,137,8,1]{1,3,2,0:T(1,128)S(1)}, u32[]{:S(2)}, u32[]{:S(2)}) collective-permute-start(f32[2,137,8,1]{1,3,2,0:T(1,128)S(1)} %get-tuple-element.37), channel_id=1, source_target_pairs={{1,0},{2,1},{3,2},{0,3},{5,4},{6,5},{7,6},{4,7},{9,8},{10,9},{11,1... | collective-permute-start | bytes 26312 | tf_op jit(solution)/shard_map/ppermute | solution.py:21
  234.3 1.0 slice-start
  235.5 6.7 %collective-permute-start.28 = (f32[2,2,137,1,64]{2,4,3,1,0:T(8,128)S(1)}, f32[2,2,137,1,64]{2,4,3,1,0:T(8,128)S(1)}, u32[]{:S(2)}, u32[]{:S(2)}) collective-permute-start(f32[2,2,137,1,64]{2,4,3,1,0:T(8,128)S(1)} %get-tuple-element.14), channel_id=1, source_target_pairs={{0,4},{4,8},{8,12},{12,16},{16,20},{20,24},{24,28},{1,5},{5,9},{9,... | collective-permute-start | bytes 420872 | tf_op jit(solution)/shard_map/ppermute | solution.py:20
  238.3 9.8 %collective-permute-start.29 = (f32[2,2,137,1,64]{2,4,3,1,0:T(8,128)S(1)}, f32[2,2,137,1,64]{2,4,3,1,0:T(8,128)S(1)}, u32[]{:S(2)}, u32[]{:S(2)}) collective-permute-start(f32[2,2,137,1,64]{2,4,3,1,0:T(8,128)S(1)} %get-tuple-element.15), channel_id=1, source_target_pairs={{4,0},{8,4},{12,8},{16,12},{20,16},{24,20},{28,24},{5,1},{9,5},{13... | collective-permute-start | bytes 420872 | tf_op jit(solution)/shard_map/ppermute | solution.py:21
  249.7 5.2 %collective-permute-start.30 = (f32[2,137,16,1]{1,3,2,0:T(1,128)S(1)}, f32[2,137,16,1]{1,3,2,0:T(1,128)S(1)}, u32[]{:S(2)}, u32[]{:S(2)}) collective-permute-start(f32[2,137,16,1]{1,3,2,0:T(1,128)S(1)} %get-tuple-element.12), channel_id=1, source_target_pairs={{0,1},{1,2},{2,3},{3,0},{4,5},{5,6},{6,7},{7,4},{8,9},{9,10},{10,1... | collective-permute-start | bytes 52616 | tf_op jit(solution)/shard_map/ppermute | solution.py:20
  251.8 3.9 %collective-permute-start.31 = (f32[2,137,16,1]{1,3,2,0:T(1,128)S(1)}, f32[2,137,16,1]{1,3,2,0:T(1,128)S(1)}, u32[]{:S(2)}, u32[]{:S(2)}) collective-permute-start(f32[2,137,16,1]{1,3,2,0:T(1,128)S(1)} %get-tuple-element.13), channel_id=1, source_target_pairs={{1,0},{2,1},{3,2},{0,3},{5,4},{6,5},{7,6},{4,7},{9,8},{10,9},{11,1... | collective-permute-start | bytes 52616 | tf_op jit(solution)/shard_map/ppermute | solution.py:21
  259.2 20.0 %copy-start.7 = (f32[1,137,16,128]{3,2,1,0:T(8,128)}, f32[1,137,16,128]{3,2,1,0:T(8,128)S(1)}, u32[]{:S(2)}) copy-start(f32[1,137,16,128]{3,2,1,0:T(8,128)S(1)} %copy.44) | copy-start | bytes 3366916
  259.2 17.0 %collective-permute-start.32 = (f32[1,137,16,128]{3,2,1,0:T(8,128)S(1)}, f32[1,137,16,128]{3,2,1,0:T(8,128)}, u32[]{:S(2)}, u32[]{:S(2)}) collective-permute-start(f32[1,137,16,128]{3,2,1,0:T(8,128)S(1)} %copy.44), channel_id=1, source_target_pairs={{0,32},{32,64},{64,96},{1,33},{33,65},{65,97},{2,34},{34,66},{66,9... | collective-permute-start | bytes 3366920 | tf_op jit(solution)/shard_map/ppermute | solution.py:29
  279.2 6.0 %copy-start.1 = (f32[32,32]{1,0:T(8,128)S(1)}, f32[32,32]{1,0:T(8,128)}, u32[]{:S(2)}) copy-start(f32[32,32]{1,0:T(8,128)} %param.7) | copy-start | bytes 12292
where the time goes:
time: 286 us; the launch traced here: 285 us
  blocking collectives  92.8 us (32%)
  starting transfers between devices  78 us (27%)
  waiting for transfers between devices  76.7 us (27%)
  local copies, waits for them, and re-layouts  18.2 us (6%)
  other arithmetic  12.1 us (4%)
  matrix products  5.61 us (2%)
    all_gather x1, blocking collectives, coarse_band(): tiles = lax.all_gather(smooth[None], ('lat', 'lon'), axis=0, tiled=True)  92.8 us
    ppermute x16, starting transfers between devices, with_halo(): before = lax.ppermute(last, axis, up)  48.7 us
    ppermute x16, waiting for transfers between devices, with_halo(): after = lax.ppermute(initial, axis, down)  38.6 us
    ppermute x16, starting transfers between devices, with_halo(): after = lax.ppermute(initial, axis, down)  27.3 us
    ppermute x16, waiting for transfers between devices, with_halo(): before = lax.ppermute(last, axis, up)  23 us
    ppermute x1, waiting for transfers between devices, shifted(): return lax.ppermute(block, axis, route)  15.1 us
  transfers between devices with their start and end apart: 33, of which 27 were waited for; matrix products, arithmetic and copies ran while one was open for 1% of the time, Pallas kernels for 0%

commit v1 on v0

v1 whole, which is shorter than its diff:
```python
import numpy as np
import jax
import jax.numpy as jnp
import ml_dtypes
from jax import lax
from jax.experimental import pallas as pl
from jax.experimental.pallas import tpu as pltpu
from jax.sharding import PartitionSpec as P

LEV, LP = 137, 144
ROWS, COLS = 16, 128
BANDS = 13
NLAT_D, NLON_D = 8, 4
MESH = pl.DeviceIdType.MESH
HIGH = lax.Precision.HIGHEST
F32, BF = jnp.float32, jnp.bfloat16

MLAT = {1: 8, 2: 4, 3: 2, 4: 1}
MLON = {1: 64, 2: 32, 3: 16, 4: 8}
DROW = {1: 0, 2: 19, 3: 30, 4: 37}
SROW = {1: 10, 2: 25, 3: 34, 4: 40}
NROWS = 42
PACK = {2: (0, 1, -1, 64), 3: (66, 2, -1, 33), 4: (101, 3, -1, 17)}
CLANE = 100
LEVEL_OF = {}
for _l in (1, 2, 3, 4):
    for _i in range(MLAT[_l] + 2):
        LEVEL_OF[DROW[_l] + _i] = (_l, "D", _i - 1)
    for _i in range(MLAT[_l] + 1):
        LEVEL_OF[SROW[_l] + _i] = (_l, "S", _i)


def lift(seq, size):
    lo, hi = min(seq), max(seq)
    zero = np.zeros(size)
    get = lambda table, i: table.get(i, zero)
    d, s = {}, {}
    for i in range(lo // 2 - 2, hi // 2 + 3):
        d[i] = get(seq, 2 * i + 1) - 0.5 * (get(seq, 2 * i) + get(seq, 2 * i + 2))
    for i in range(lo // 2 - 2, hi // 2 + 3):
        s[i] = get(seq, 2 * i) + 0.25 * (get(d, i - 1) + get(d, i))
    keep = lambda table: {i: v for i, v in table.items() if np.any(v)}
    return keep(s), keep(d)


def message_lanes():
    left, right = {}, {}
    nl = nr = 0
    for j in range(NROWS):
        l, kind, _ = LEVEL_OF[j]
        ql = ["dm1"] if l == 1 else (["sm", "dm1", "dm"] if kind == "D" else ["dm1", "dm"])
        qr = ["d-1", "d0"] if (l == 1 or kind == "S") else ["s0", "d-1", "d0"]
        left[j], right[j] = (nl, ql), (nr, qr)
        nl, nr = nl + len(ql), nr + len(qr)
    assert nl <= CLANE and nr <= CLANE
    return left, right


LEFT, RIGHT = message_lanes()


def lon_tables():
    raw = {i: np.eye(256)[i] for i in range(COLS)}
    smooth, detail = {0: raw}, {}
    for l in range(1, 5):
        smooth[l], detail[l] = lift(smooth[l - 1], 256)
    ext_s = {}
    for l in (2, 3, 4):
        at, depth, lo, hi = PACK[l]
        seq = {i: np.eye(256)[128 + at + i - lo] for i in range(lo, hi + 1)}
        for k in range(l, 5):
            s, d = lift(seq, 256)
            seq = s
            ext_s[l, k] = (s, d)
    zero = np.zeros(256)
    full_s, full_d = {}, {}
    for k in range(1, 5):
        s, d = dict(smooth[k]), dict(detail[k])
        for l in range(2, k + 1):
            for table, more in ((s, ext_s[l, k][0]), (d, ext_s[l, k][1])):
                for i, v in more.items():
                    table[i] = table.get(i, zero) + v
        full_s[k], full_d[k] = s, d
    return smooth, full_s, full_d


def constants():
    smooth, fs, fd = lon_tables()
    zero = np.zeros(256)
    out = {}
    for l in (1, 2, 3, 4):
        m = MLON[l]
        w = np.zeros((256, 256))
        off = 128 if l == 1 else 64
        for i in range(0, m + 1):
            w[:, i] = fs[l].get(i, zero)
        for i in range(-1, m + 1):
            w[:, off + i + 1] = fd[l].get(i, zero)
        out["W", l] = w if l == 1 else w[:, :128]
        g = np.zeros((256, 256))
        pick = {"sm": fs[l].get(m, zero), "dm1": fd[l].get(m - 1, zero), "dm": fd[l].get(m, zero),
                "s0": fs[l].get(0, zero), "d-1": fd[l].get(-1, zero), "d0": fd[l].get(0, zero)}
        z = np.zeros((256, 256))
        for j in range(NROWS):
            if LEVEL_OF[j][0] != l:
                continue
            smooth_too = LEVEL_OF[j][1] == "D"
            for base, (at, names) in ((0, LEFT[j]), (128, RIGHT[j])):
                for q, name in enumerate(names):
                    lane = base + at + q
                    g[:, lane] = pick[name]
                    row = z[lane]
                    if base == 0:
                        if name == "dm1":
                            row[off + 0] += 1.0
                            if l == 1 and smooth_too:
                                row[0] += 0.25
                        if name == "dm":
                            row[off + 1] += 1.0
                            if smooth_too:
                                row[1] += 0.25
                        if name == "sm":
                            row[0] += 1.0
                    else:
                        if name == "s0":
                            row[m] += 1.0
                        if name == "d-1":
                            row[off + m] += 1.0
                            if smooth_too:
                                row[m - 1] += 0.25
                                if l == 1:
                                    row[m] += -1.75
                        if name == "d0":
                            row[off + m + 1] += 1.0
                            if l == 1 and smooth_too:
                                row[m] += 0.25
        out["G", l] = g
        out["Z", l] = z if l == 1 else z[:, :128]
        n_in = 256 if l == 1 else 128
        eye = np.eye(n_in)
        s = {i: eye[i] for i in range(0, m + 1)}
        d = {i: eye[off + i + 1] for i in range(-1, m + 1)}
        e = {i: s[i] - 0.25 * (d[i - 1] + d[i]) for i in range(0, m + 1)}
        t = np.zeros((n_in, 128))
        for i in range(0, m + 1):
            if 2 * i < 128:
                t[:, 2 * i] = e[i]
            if i < m:
                t[:, 2 * i + 1] = d[i] + 0.5 * (e[i] + e[i + 1])
        out["T", l] = t
    for l in (2, 3, 4):
        at, depth, lo, hi = PACK[l]
        sm = np.zeros((128, 128))
        for i in range(lo, hi + 1):
            sm[:, at + i - lo] = smooth[depth][i][:128]
        out["Sm", l] = sm
    m4 = np.zeros((128, 128))
    for lane in range(88):
        m4[:, lane] = smooth[4][lane % 11 - 1][:128]
    out["M4", 0] = m4
    sel = np.zeros((256, 256))
    for rho in range(2):
        for g in range(2):
            for i in range(4):
                for c in range(11):
                    sel[128 * rho + g * 44 + i * 11 + c, 128 * g + CLANE + 11 * rho + c] = 1.0
    out["Sel", 0] = sel
    return out


CONST = constants()


def pack_constants():
    tiles, where = [], {}

    def put(key, a):
        k, n = a.shape
        where[key] = (sum(t.shape[0] for t in tiles), k, n)
        if n < 256:
            a = np.concatenate([a, np.zeros((k, 256 - n), a.dtype)], 1)
        tiles.append(a)

    for key, a in CONST.items():
        if key == ("W", 1) or key == ("G", 1):
            a = a[:128]
        hi = a.astype(ml_dtypes.bfloat16)
        lo = (a - hi.astype(np.float64)).astype(ml_dtypes.bfloat16)
        put(key + ("hi",), hi)
        if np.any(lo.astype(np.float64)):
            put(key + ("lo",), lo)
    return np.concatenate(tiles, 0), where


CB, CWHERE = pack_constants()


def ext_coefficients():
    syms = {("U", 2): 0, ("U", 3): 1, ("U", 4): 2, ("W", 2): 3, ("W", 3): 4, ("W", 4): 5}
    unit = lambda key: np.eye(6)[syms[key]]
    zero = np.zeros(6)
    s = {i: zero for i in range(9)}
    table = {}
    for l in (2, 3, 4):
        m = MLAT[l]
        d = {-1: unit(("U", l)), m: unit(("W", l))}
        for i in range(m):
            d[i] = s[2 * i + 1] - 0.5 * (s[2 * i] + s[2 * i + 2])
        s = {i: s[2 * i] + 0.25 * (d[i - 1] + d[i]) for i in range(m + 1)}
        for i in range(-1, m + 1):
            table[DROW[l] + i + 1] = d[i]
        for i in range(m + 1):
            table[SROW[l] + i] = s[i]
    out = np.zeros((48, 128), np.float32)
    for j, v in table.items():
        for l in (2, 3, 4):
            at, _, lo, hi = PACK[l]
            out[j - 19, at:at + hi - lo + 1] = v[l - 2]
            out[24 + j - 19, at:at + hi - lo + 1] = v[3 + l - 2]
    return out


def gather_expand():
    out = np.zeros((8, 1024), np.float32)
    for a in range(8):
        for lane in range(88):
            col = a + (lane // 11) % 4 - 1
            if 0 <= col < 8:
                out[col, a * 128 + lane] = 1.0
    return out


EXT = ext_coefficients()
EXPAND = gather_expand()


def split(a):
    hi = a.astype(BF)
    return hi, (a - hi.astype(F32)).astype(BF)


def dot(a, b):
    return jnp.dot(a, b, preferred_element_type=F32)


def kernel(x, vert, latf, lonf, cb, ext_c, expand, inc, jump,
           xs, so, rw, lx, up, dn, p2, cm, r_w, r_u, r_pw, r_pu, r_p2u, r_p2w, cbuf,
           vst, vtmp, cf, qm, o1, o2, tmsg, s_l, s_r, s_o, m_l, m_r, m_o,
           bd, sm, ys, prev, send, recv):
    tm, lat, lon = lax.axis_index("tm"), lax.axis_index("lat"), lax.axis_index("lon")
    mu = (lat > 0).astype(F32)
    mw = (lat < NLAT_D - 1).astype(F32)
    mu2 = (lat > 1).astype(F32)
    mw2 = (lat < NLAT_D - 2).astype(F32)

    def at_lat(k):
        return (tm, lax.rem(lat + k + NLAT_D, NLAT_D), lon)

    def at_lon(k):
        return (tm, lat, lax.rem(lon + k + NLON_D, NLON_D))

    def at_tm(k):
        return (lax.rem(tm + k + 4, 4), lat, lon)

    partners = [at_lat(k) for k in range(1, 8)] + [at_lon(k) for k in range(1, 4)] + [at_tm(1), at_tm(-1)]
    barrier = pltpu.get_barrier_semaphore()
    for p in partners:
        pl.semaphore_signal(barrier, inc=1, device_id=p, device_id_type=MESH)

    def const(key):
        at, k, n = CWHERE[key]
        return cb[at:at + k, 0:n]

    def mm(a, name, l):
        hi, lo = split(a)
        w = const((name, l, "hi"))
        out = dot(hi, w) + dot(lo, w)
        if (name, l, "lo") in CWHERE:
            out = out + dot(hi, const((name, l, "lo")))
        return out

    for r in range(ROWS):
        xs[r, 136:144, :] = jnp.zeros((8, COLS), F32)
        xs[r, 0:LEV, :] = x[pl.ds(r, LEV, stride=ROWS), :]

    for i in range(7):
        rw[1 + i] = xs[2 * i + 1] - 0.5 * (xs[2 * i] + xs[2 * i + 2])
    dn[0] = xs[15] - 0.5 * xs[14]
    up[0] = xs[0]
    up[1] = rw[1]

    pl.semaphore_wait(barrier, len(partners))
    sems = iter(range(64))

    def remote(src, dst, dev, slot=None):
        k = next(sems)
        return pltpu.make_async_remote_copy(
            src_ref=src, dst_ref=dst, send_sem=send.at[k],
            recv_sem=recv.at[k], device_id=dev, device_id_type=MESH)

    copies = []

    def go(c):
        c.start()
        copies.append(c)

    go(remote(up.at[pl.ds(0, 2)], r_w, at_lat(-1)))
    go(remote(dn.at[0], r_u, at_lat(1)))

    so[0] = (-0.125 * mu) * xs[0]
    so[1] = 0.875 * xs[0] + 0.25 * rw[1]
    for i in range(1, 7):
        so[1 + i] = xs[2 * i] + 0.25 * (rw[i] + rw[1 + i])
    so[8] = xs[14] + 0.25 * (rw[7] + dn[0])
    so[9] = (0.25 * mw) * dn[0]
    sbase = {1: 0, 2: 10, 3: 17, 4: 22}
    dbase = {2: 26, 3: 32, 4: 36}
    for l in (2, 3, 4):
        m, a, b, d = MLAT[l], sbase[l - 1], sbase[l], dbase[l]
        S = lambda i: so[a + 1 + i]
        so[d] = S(-1) - 0.5 * S(0)
        for i in range(m):
            so[d + 1 + i] = S(2 * i + 1) - 0.5 * (S(2 * i) + S(2 * i + 2))
        so[d + 1 + m] = (-0.5 * S(2 * m)) if l == 2 else S(2 * m + 1) - 0.5 * S(2 * m)
        so[b] = (0.25 * mu) * so[d]
        for i in range(m):
            so[b + 1 + i] = S(2 * i) + 0.25 * (so[d + i] + so[d + 1 + i])
        so[b + 1 + m] = mw * (S(2 * m) + 0.25 * (so[d + m] + so[d + 1 + m]))
        so[b + 2 + m] = (0.25 * mw) * so[d + 1 + m]
    d4 = mm(so[37], "Sm", 4)
    up[2] = mm(so[27], "Sm", 2) + mm(so[33], "Sm", 3) + d4
    dn[1] = mm(so[30], "Sm", 2) + mm(so[34], "Sm", 3) + d4
    p2[0] = mm(so[38], "Sm", 4)
    p2[1] = mm(so[36], "Sm", 4)
    go(remote(up.at[2], r_pw, at_lat(-1)))
    go(remote(dn.at[1], r_pu, at_lat(1)))
    go(remote(p2.at[0], r_p2u, at_lat(2)))
    go(remote(p2.at[1], r_p2w, at_lat(-2)))
    lane = lax.broadcasted_iota(jnp.int32, (1, 128), 1)
    half = LP // 2
    acc = jnp.zeros((half, 128), F32)
    for i in range(4):
        t = mm(so[22 + i], "M4", 0)
        for g in range(2):
            lo = g * 44 + i * 11
            acc = jnp.where((lane >= lo) & (lane < lo + 11), t[g * half:(g + 1) * half], acc)
    cbuf[lat] = acc
    cm[...] = acc
    for k in range(1, 8):
        go(remote(cm, cbuf.at[lat], at_lat(k)))

    vtmp[...] = jnp.zeros((LP, 256), F32)
    for k in range(BANDS):
        vtmp[0:LEV, 0:LEV] = vert[k]
        hi, lo = split(vtmp[...])
        vst[k, 0:LP, :] = hi
        vst[k, LP:2 * LP, :] = lo
    cf[...] = jnp.zeros((16, 1024), F32)
    cf[0:8, :] = jnp.dot(latf[...], expand[...], precision=HIGH, preferred_element_type=F32)
    rowi = lax.broadcasted_iota(jnp.int32, (128, 32), 0)
    coli = lax.broadcasted_iota(jnp.int32, (128, 32), 1)
    place = ((rowi <= 8) & (coli == lax.rem(8 * lon + rowi, 32))).astype(F32)
    ylon = jnp.dot(place, lonf[...], precision=HIGH, preferred_element_type=F32)
    for rho in range(2):
        for n, delta in enumerate((0, -1, 1, 2)):
            c = rowi - (CLANE + 11 * rho)
            pick = ((c >= 0) & (c < 11) & (coli == lax.rem(8 * lon + 8 * delta + 63 + c, 32))).astype(F32)
            q = lax.dot_general(pick, ylon, (((1,), (1,)), ((), ())), precision=HIGH,
                                preferred_element_type=F32)
            hi, lo = split(q)
            qm[0, n * 128:(n + 1) * 128, rho * 128:(rho + 1) * 128] = hi
            qm[1, n * 128:(n + 1) * 128, rho * 128:(rho + 1) * 128] = lo

    for c in copies:
        c.wait()
    copies.clear()

    x16 = lambda: mw * r_w[0]
    rw[0] = mu * r_u[...] - 0.5 * xs[0]
    rw[8] = dn[0] - 0.5 * x16()
    rw[9] = mw * r_w[1]
    for i in range(8):
        rw[10 + i] = xs[2 * i] + 0.25 * (rw[i] + rw[i + 1])
    rw[18] = x16() + (0.25 * mw) * (rw[8] + rw[9])
    raw = lambda j: rw[j] if j < 19 else lx[j - 19, :, 0:128]
    for l in (2, 3, 4):
        m, a, d, b = MLAT[l], SROW[l - 1], DROW[l], SROW[l]
        lx[d - 19, :, 0:128] = so[dbase[l]]
        lx[d + m + 1 - 19, :, 0:128] = so[dbase[l] + m + 1]
        for i in range(m):
            lx[d + 1 + i - 19, :, 0:128] = raw(a + 2 * i + 1) - 0.5 * (raw(a + 2 * i) + raw(a + 2 * i + 2))
        for i in range(m + 1):
            v = raw(a + 2 * i) + 0.25 * (raw(d + i) + raw(d + i + 1))
            lx[b + i - 19, :, 0:128] = mw * v if i == m else v
    r_pu[...] = mu * r_pu[...] + mu2 * r_p2u[...]
    r_pw[...] = mw * r_pw[...] + mw2 * r_p2w[...]
    for j in range(19, NROWS):
        cu, cw = ext_c[j - 19:j - 18, :], ext_c[24 + j - 19:24 + j - 18, :]
        l, kind, i = LEVEL_OF[j]
        if kind == "S" and i == MLAT[l]:
            cu, cw = cu * mw, cw * mw
        lx[j - 19, :, 128:256] = r_pu[...] * cu + r_pw[...] * cw
    rw[0] = mu * rw[0]
    for l in (2, 3, 4):
        lx[DROW[l] - 19] = mu * lx[DROW[l] - 19]

    tt = []
    for rho in range(2):
        c = cf[pl.ds(lat + rho, 1), :]
        tt.append(sum(cbuf[a] * c[:, a * 128:(a + 1) * 128] for a in range(8)))
    u2 = mm(jnp.concatenate(tt, axis=1), "Sel", 0)
    s_o[0:half, :] = u2[:, 0:128]
    s_o[half:LP, :] = u2[:, 128:256]

    groups = {1: (0, 19), 2: (19, 30), 3: (30, 37), 4: (37, 42)}

    def operand(l):
        lo, hi = groups[l]
        if l == 1:
            return rw[...].reshape(19 * LP, 128)
        return lx[lo - 19:hi - 19].reshape((hi - lo) * LP, 256)

    s_l[...] = s_o[...]
    s_r[...] = s_o[...]
    for l in (1, 2, 3, 4):
        lo, hi = groups[l]
        tmsg[0:hi - lo] = mm(operand(l), "G", l).reshape(hi - lo, LP, 256)
        for dst, table, base in ((s_l, LEFT, 0), (s_r, RIGHT, 128)):
            v = dst[...]
            for j in range(lo, hi):
                at, names = table[j]
                v = jnp.where((lane >= at) & (lane < at + len(names)), tmsg[j - lo, :, base:base + 128], v)
            dst[...] = v
    go(remote(s_l, m_l, at_lon(1)))
    go(remote(s_r, m_r, at_lon(-1)))
    go(remote(s_o, m_o, at_lon(2)))

    o1[...] = mm(operand(1), "W", 1).reshape(19, LP, 256)
    for l in (2, 3, 4):
        lo, hi = groups[l]
        o2[lo - 19:hi - 19] = mm(operand(l), "W", l).reshape(hi - lo, LP, 128)

    for c in copies:
        c.wait()
    copies.clear()

    rl_hi, rl_lo = split(m_l[...])
    rr_hi, rr_lo = split(m_r[...])
    rhi = jnp.concatenate([rl_hi, rr_hi], axis=1).astype(F32)
    rlo = jnp.concatenate([rl_lo, rr_lo], axis=1).astype(F32)
    lane2 = lax.broadcasted_iota(jnp.int32, (1, 256), 1)

    def received(j):
        (al, nl), (ar, nr) = LEFT[j], RIGHT[j]
        keep = ((lane2 >= al) & (lane2 < al + len(nl))) | ((lane2 >= 128 + ar) & (lane2 < 128 + ar + len(nr)))
        keep = keep.astype(F32)
        return jnp.concatenate([(rhi * keep).astype(BF), (rlo * keep).astype(BF)], axis=0)

    def vmul(ks, t):
        hi, lo = split(t)
        both = jnp.concatenate([hi, lo], axis=1)
        outs = []
        for k in ks:
            p = dot(vst[k][:, 0:LP], both)
            outs.append(p[0:LP, 0:128] + p[0:LP, 128:256] + p[LP:2 * LP, 0:128])
        return outs

    low = lane < 64
    z1 = const(("Z", 1, "hi"))
    for j in range(0, 19):
        if j < 10:
            p = dot(received(j), z1)
            t = o1[j] + p[0:LP] + p[LP:2 * LP]
            bd[42 + j] = vmul((1,), t[:, 0:128])[0]
            bd[j] = vmul((2,), t[:, 128:256])[0]
        else:
            p = dot(received(j), z1[:, 128:256])
            bd[j] = vmul((0,), o1[j, :, 128:256] + p[0:LP] + p[LP:2 * LP])[0]
    for l in (2, 3, 4):
        z = const(("Z", l, "hi"))
        for j in range(*groups[l]):
            p = dot(received(j), z)
            t = o2[j - 19] + p[0:LP] + p[LP:2 * LP]
            if LEVEL_OF[j][1] == "D":
                a, b = vmul((3 * l - 2, 3 * l - 1), t)
                bd[j] = jnp.where(low, a, b)
            else:
                bd[j] = jnp.where(low, 0.0, vmul((3 * l - 3,), t)[0])

    uhi, ulo = split(jnp.concatenate([s_o[...], m_l[...], m_r[...], m_o[...]], axis=1))
    c = dot(uhi, qm[0]) + dot(ulo, qm[0]) + dot(uhi, qm[1])
    for rho in range(2):
        v = vmul((BANDS - 1,), c[:, rho * 128:(rho + 1) * 128])[0]
        sm[rho] = v * mw if rho else v

    for l in (4, 3, 2):
        m, d, b = MLAT[l], DROW[l], SROW[l]
        for i in range(m + 1):
            s = bd[b + i] + sm[i]
            sm[i] = s - 0.25 * (bd[d + i] + bd[d + i + 1])
        for i in range(2 * m, -1, -1):
            if i % 2:
                h = i // 2
                tmsg[i, :, 0:128] = bd[d + 1 + h] + 0.5 * (sm[h] + sm[h + 1])
            else:
                tmsg[i, :, 0:128] = sm[i // 2]
        n = 2 * m + 1
        out = mm(tmsg[0:n, :, 0:128].reshape(n * LP, 128), "T", l).reshape(n, LP, 128)
        sm[0:n] = out
        sm[2 * m] = mw * sm[2 * m]
    for i in range(9):
        tmsg[2 * i, :, 0:128] = sm[i] - 0.25 * (bd[42 + i] + bd[43 + i])
        tmsg[2 * i, :, 128:256] = bd[10 + i] - 0.25 * (bd[i] + bd[i + 1])
    for i in range(8):
        tmsg[2 * i + 1, :, 0:128] = bd[43 + i] + 0.5 * (tmsg[2 * i, :, 0:128] + tmsg[2 * i + 2, :, 0:128])
        tmsg[2 * i + 1, :, 128:256] = bd[1 + i] + 0.5 * (tmsg[2 * i, :, 128:256] + tmsg[2 * i + 2, :, 128:256])
    for q in range(4):
        y = mm(tmsg[4 * q:4 * q + 4].reshape(4 * LP, 256), "T", 1).reshape(4, LP, 128)
        ys[4 * q:4 * q + 4] = y
        go(remote(ys.at[pl.ds(4 * q, 4)], prev.at[pl.ds(4 * q, 4)], at_tm(1)))
    for r in range(ROWS):
        inc[pl.ds(r, LEV, stride=ROWS), :] = ys[r, 0:LEV, :]
    first = (tm > 0).astype(F32)
    for q in range(4):
        copies[q].wait()
        for r in range(4 * q, 4 * q + 4):
            jump[pl.ds(r, LEV, stride=ROWS), :] = ys[r, 0:LEV, :] - first * prev[r, 0:LEV, :]


def body(forcing, vertical, lat_factor, lon_factor):
    x = forcing.reshape(LEV * ROWS, COLS)
    tile = (LP, 128)
    vm = pl.BlockSpec(memory_space=pltpu.VMEM)
    S = pltpu.VMEM
    scratch = [
        S((ROWS,) + tile, F32), S((39,) + tile, F32), S((19,) + tile, F32), S((23, LP, 256), F32),
        S((3,) + tile, F32), S((2,) + tile, F32), S((2,) + tile, F32), S((LP // 2, 128), F32),
        S((2,) + tile, F32), S(tile, F32), S(tile, F32), S(tile, F32), S(tile, F32), S(tile, F32),
        S((8, LP // 2, 128), F32),
        S((BANDS, 2 * LP, 256), BF), S((LP, 256), F32), S((16, 1024), F32), S((2, 512, 256), BF),
        S((19, LP, 256), F32), S((23,) + tile, F32), S((19, LP, 256), F32),
        S(tile, F32), S(tile, F32), S(tile, F32), S(tile, F32), S(tile, F32), S(tile, F32),
        S((52,) + tile, F32), S((9,) + tile, F32), S((ROWS,) + tile, F32), S((ROWS,) + tile, F32),
        pltpu.SemaphoreType.DMA((24,)), pltpu.SemaphoreType.DMA((24,)),
    ]
    out = jax.ShapeDtypeStruct((LEV * ROWS, COLS), F32)
    inc, jump = pl.pallas_call(
        kernel,
        out_shape=(out, out),
        in_specs=[vm] * 7,
        out_specs=(vm, vm),
        scratch_shapes=scratch,
        compiler_params=pltpu.CompilerParams(
            collective_id=0, has_side_effects=True, vmem_limit_bytes=56 * 1024 * 1024),
    )(x, vertical, lat_factor, lon_factor, jnp.asarray(CB), jnp.asarray(EXT), jnp.asarray(EXPAND))
    shape = (1, LEV, ROWS, COLS)
    return inc.reshape(shape), jump.reshape(shape)


def solution(mesh):
    placed = (P("tm", None, "lat", "lon"), P(), P(), P())
    return jax.shard_map(
        body,
        mesh=mesh,
        in_specs=placed,
        out_specs=(P("tm", None, "lat", "lon"), P("tm", None, "lat", "lon")),
        check_vma=False,
    )
```

time: 286 us -> 57.3 us (0.20)
  blocking collectives: 92.8 us -> 0 us
  starting transfers between devices: 78 us -> 0 us
  waiting for transfers between devices: 76.7 us -> 0 us
  Pallas kernels: 0 us -> 52.1 us
  local copies, waits for them, and re-layouts: 18.2 us -> 3.41 us
  other arithmetic: 12.1 us -> 0 us
  matrix products: 5.61 us -> 0 us
    all_gather x1 -> x0, blocking collectives: 92.8 us -> none  [coarse_band(): tiles = lax.all_gather(smooth[None], ('lat', 'lon'), axis=0, tiled=True)]
    ppermute x33 -> x0, starting transfers between devices: 78 us -> none  [the longest x16 48.7 us: with_halo(): before = lax.ppermute(last, axis, up)]
    ppermute x33 -> x0, waiting for transfers between devices: 76.7 us -> none  [the longest x16 38.6 us: with_halo(): after = lax.ppermute(initial, axis, down)]
    pallas_call x0 -> x1, Pallas kernels: none -> 52.1 us  [body(): pl.pallas_call(kernel, out_shape=(out, out), in_specs=[vm] * 7, out_specs...]
    slice x27 -> x0, local copies, waits for them, and re-layouts: 6.13 us -> none  [the longest x12 4.87 us: cut(): return lax.slice_in_dim(field, start, stop, stride, axis)]
    sub x17 -> x0, other arithmetic: 5.72 us -> none  [the longest x1 3.2 us: body(): return (increment, increment - earlier)]
    dot_general x7 -> x0, matrix products: 5.61 us -> none  [the longest x4 4 us: covary(): jnp.einsum('bij,bjxy->bixy', vertical[3 * level:3 * level + 3], details,...]
    concatenate x16 -> x0, other arithmetic: 3.15 us -> none  [with_halo(): shard = jnp.concatenate([before, shard, after], axis=dim)]
  transfers between devices with their start and end apart: 33 -> 0, of which waited for: 27 -> 0; matrix products, arithmetic and copies ran while one was open for 1% -> 0% of each run, Pallas kernels for 0% -> 0%
where the time goes in v1:
time: 57.3 us; the launch traced here: 56.2 us
  Pallas kernels  52.1 us (91%)
  local copies, waits for them, and re-layouts  3.41 us (6%)
  between operations  0.65 us (1%)
    pallas_call x1, Pallas kernels, body(): pl.pallas_call(kernel, out_shape=(out, out), in_specs=[vm] * 7, out_specs...  52.1 us
    unnamed x4, local copies, waits for them, and re-layouts  3.41 us

profile of v1, /device:TPU:2, one launch (start us, length us, event | category | flops | bytes accessed | tf_op | source)
XLA Modules:
  0.0 56.2 jit_solution(13441163606583772455)
XLA Ops:
  0.6 52.1 %shard_map.86 = (f32[2192,128]{1,0:T(8,128)}, f32[2192,128]{1,0:T(8,128)}) custom-call(f32[2192,128]{1,0:T(8,128)} %bitcast.3, f32[13,137,137]{2,1,0:T(8,128)} %vert.1, f32[8,8]{1,0:T(8,128)} %latf.1, f32[32,32]{1,0:T(8,128)} %lonf.1, bf16[4864,256]{1,0:T(8,128)(2,1)} %constant.6.clone.cb, f32[48,128]{1,0:T(8,128)} %constant.7.clone.ext_c, ...), custom_call_target="tpu_custom_call" | custom-call | tf_op jit(solution)/shard_map/pallas_call | solution.py:547
  52.8 0.0 copy-start
  52.8 2.4 %copy.11 = f32[1,137,16,128]{3,2,1,0:T(8,128)} copy(f32[1,137,16,128]{3,2,1,0:T(8,128)} %bitcast.5) | data formatting | bytes 2244608
  55.2 0.0 copy-done
  55.2 1.0 %copy.12 = f32[1,137,16,128]{3,2,1,0:T(8,128)} copy(f32[1,137,16,128]{3,2,1,0:T(8,128)S(1)} %bitcast.4) | data formatting | bytes 2244608
Async XLA Ops:
  52.8 2.4 %copy-start = (f32[2192,128]{1,0:T(8,128)S(1)}, f32[2192,128]{1,0:T(8,128)}, u32[]{:S(2)}) copy-start(f32[2192,128]{1,0:T(8,128)} %get-tuple-element.5) | copy-start | bytes 3366916

commit v2 on v1

--- a/solution.py
+++ b/solution.py
@@ -21,7 +21,8 @@
 SROW = {1: 10, 2: 25, 3: 34, 4: 40}
 NROWS = 42
 PACK = {2: (0, 1, -1, 64), 3: (66, 2, -1, 33), 4: (101, 3, -1, 17)}
-CLANE = 100
+FOLD, WIDE = 16, 9
+FOLD_LANES = LP // FOLD * WIDE
 LEVEL_OF = {}
 for _l in (1, 2, 3, 4):
     for _i in range(MLAT[_l] + 2):
@@ -52,7 +53,7 @@
         qr = ["d-1", "d0"] if (l == 1 or kind == "S") else ["s0", "d-1", "d0"]
         left[j], right[j] = (nl, ql), (nr, qr)
         nl, nr = nl + len(ql), nr + len(qr)
-    assert nl <= CLANE and nr <= CLANE
+    assert nl <= 128 and nr <= 128
     return left, right
 
 
@@ -154,17 +155,10 @@
         for i in range(lo, hi + 1):
             sm[:, at + i - lo] = smooth[depth][i][:128]
         out["Sm", l] = sm
-    m4 = np.zeros((128, 128))
-    for lane in range(88):
-        m4[:, lane] = smooth[4][lane % 11 - 1][:128]
-    out["M4", 0] = m4
-    sel = np.zeros((256, 256))
-    for rho in range(2):
-        for g in range(2):
-            for i in range(4):
-                for c in range(11):
-                    sel[128 * rho + g * 44 + i * 11 + c, 128 * g + CLANE + 11 * rho + c] = 1.0
-    out["Sel", 0] = sel
+    c4 = np.zeros((256, 128))
+    for c in range(11):
+        c4[:, c] = fs[4].get(c - 1, zero)
+    out["C4", 0] = c4
     return out
 
 
@@ -220,18 +214,7 @@
     return out
 
 
-def gather_expand():
-    out = np.zeros((8, 1024), np.float32)
-    for a in range(8):
-        for lane in range(88):
-            col = a + (lane // 11) % 4 - 1
-            if 0 <= col < 8:
-                out[col, a * 128 + lane] = 1.0
-    return out
-
-
 EXT = ext_coefficients()
-EXPAND = gather_expand()
 
 
 def split(a):
@@ -243,10 +226,11 @@
     return jnp.dot(a, b, preferred_element_type=F32)
 
 
-def kernel(x, vert, latf, lonf, cb, ext_c, expand, inc, jump,
-           xs, so, rw, lx, up, dn, p2, cm, r_w, r_u, r_pw, r_pu, r_p2u, r_p2w, cbuf,
-           vst, vtmp, cf, qm, o1, o2, tmsg, s_l, s_r, s_o, m_l, m_r, m_o,
-           bd, sm, ys, prev, send, recv):
+def kernel(x_hbm, vert_hbm, latf_hbm, lonf_hbm, cb_hbm, ext_hbm, inc_hbm, jump_hbm,
+           x, vert, latf, lonf, cb, ext_c, inc, jump,
+           xs, so, rw, lx, up, dn, p2, r_w, r_u, r_pw, r_pu, r_p2u, r_p2w,
+           vst, vtmp, pm, o1, o2, tmsg, s_l, s_r, m_l, m_r, sf, mf, cbuf,
+           bd, sm, ys, prev, send, recv, load):
     tm, lat, lon = lax.axis_index("tm"), lax.axis_index("lat"), lax.axis_index("lon")
     mu = (lat > 0).astype(F32)
     mw = (lat < NLAT_D - 1).astype(F32)
@@ -266,6 +250,13 @@
     barrier = pltpu.get_barrier_semaphore()
     for p in partners:
         pl.semaphore_signal(barrier, inc=1, device_id=p, device_id_type=MESH)
+
+    loads = {}
+    for n, (name, src, dst) in enumerate((("x", x_hbm, x), ("cb", cb_hbm, cb), ("ext", ext_hbm, ext_c),
+                                          ("lonf", lonf_hbm, lonf), ("latf", latf_hbm, latf),
+                                          ("vert", vert_hbm, vert))):
+        loads[name] = pltpu.make_async_copy(src, dst, load.at[n])
+        loads[name].start()
 
     def const(key):
         at, k, n = CWHERE[key]
@@ -279,6 +270,7 @@
             out = out + dot(hi, const((name, l, "lo")))
         return out
 
+    loads["x"].wait()
     for r in range(ROWS):
         xs[r, 136:144, :] = jnp.zeros((8, COLS), F32)
         xs[r, 0:LEV, :] = x[pl.ds(r, LEV, stride=ROWS), :]
@@ -289,7 +281,6 @@
     up[0] = xs[0]
     up[1] = rw[1]
 
-    pl.semaphore_wait(barrier, len(partners))
     sems = iter(range(64))
 
     def remote(src, dst, dev, slot=None):
@@ -303,9 +294,6 @@
     def go(c):
         c.start()
         copies.append(c)
-
-    go(remote(up.at[pl.ds(0, 2)], r_w, at_lat(-1)))
-    go(remote(dn.at[0], r_u, at_lat(1)))
 
     so[0] = (-0.125 * mu) * xs[0]
     so[1] = 0.875 * xs[0] + 0.25 * rw[1]
@@ -327,49 +315,41 @@
             so[b + 1 + i] = S(2 * i) + 0.25 * (so[d + i] + so[d + 1 + i])
         so[b + 1 + m] = mw * (S(2 * m) + 0.25 * (so[d + m] + so[d + 1 + m]))
         so[b + 2 + m] = (0.25 * mw) * so[d + 1 + m]
+    loads["cb"].wait()
     d4 = mm(so[37], "Sm", 4)
     up[2] = mm(so[27], "Sm", 2) + mm(so[33], "Sm", 3) + d4
     dn[1] = mm(so[30], "Sm", 2) + mm(so[34], "Sm", 3) + d4
     p2[0] = mm(so[38], "Sm", 4)
     p2[1] = mm(so[36], "Sm", 4)
+    pl.semaphore_wait(barrier, len(partners))
+    go(remote(up.at[pl.ds(0, 2)], r_w, at_lat(-1)))
+    go(remote(dn.at[0], r_u, at_lat(1)))
     go(remote(up.at[2], r_pw, at_lat(-1)))
     go(remote(dn.at[1], r_pu, at_lat(1)))
     go(remote(p2.at[0], r_p2u, at_lat(2)))
     go(remote(p2.at[1], r_p2w, at_lat(-2)))
     lane = lax.broadcasted_iota(jnp.int32, (1, 128), 1)
-    half = LP // 2
-    acc = jnp.zeros((half, 128), F32)
-    for i in range(4):
-        t = mm(so[22 + i], "M4", 0)
-        for g in range(2):
-            lo = g * 44 + i * 11
-            acc = jnp.where((lane >= lo) & (lane < lo + 11), t[g * half:(g + 1) * half], acc)
-    cbuf[lat] = acc
-    cm[...] = acc
-    for k in range(1, 8):
-        go(remote(cm, cbuf.at[lat], at_lat(k)))
-
+
+    for name in ("ext", "lonf", "latf", "vert"):
+        loads[name].wait()
     vtmp[...] = jnp.zeros((LP, 256), F32)
     for k in range(BANDS):
         vtmp[0:LEV, 0:LEV] = vert[k]
         hi, lo = split(vtmp[...])
         vst[k, 0:LP, :] = hi
         vst[k, LP:2 * LP, :] = lo
-    cf[...] = jnp.zeros((16, 1024), F32)
-    cf[0:8, :] = jnp.dot(latf[...], expand[...], precision=HIGH, preferred_element_type=F32)
     rowi = lax.broadcasted_iota(jnp.int32, (128, 32), 0)
     coli = lax.broadcasted_iota(jnp.int32, (128, 32), 1)
-    place = ((rowi <= 8) & (coli == lax.rem(8 * lon + rowi, 32))).astype(F32)
-    ylon = jnp.dot(place, lonf[...], precision=HIGH, preferred_element_type=F32)
-    for rho in range(2):
-        for n, delta in enumerate((0, -1, 1, 2)):
-            c = rowi - (CLANE + 11 * rho)
-            pick = ((c >= 0) & (c < 11) & (coli == lax.rem(8 * lon + 8 * delta + 63 + c, 32))).astype(F32)
-            q = lax.dot_general(pick, ylon, (((1,), (1,)), ((), ())), precision=HIGH,
-                                preferred_element_type=F32)
-            hi, lo = split(q)
-            qm[0, n * 128:(n + 1) * 128, rho * 128:(rho + 1) * 128] = hi
-            qm[1, n * 128:(n + 1) * 128, rho * 128:(rho + 1) * 128] = lo
+    mine = ((rowi < 11) & (coli == lax.rem(8 * lon + 31 + rowi, 32))).astype(F32)
+    for k in range(NLON_D):
+        theirs = (rowi < FOLD_LANES) & (coli == lax.rem(8 * (lon + k) + lax.rem(rowi, WIDE), 32))
+        part = jnp.dot(theirs.astype(F32), lonf[...], precision=HIGH, preferred_element_type=F32)
+        part = lax.dot_general(mine, part, (((1,), (1,)), ((), ())), precision=HIGH,
+                               preferred_element_type=F32)
+        c4 = const(("C4", 0, "hi")).astype(F32) + const(("C4", 0, "lo")).astype(F32)
+        hi, lo = split(jnp.dot(c4, part, precision=HIGH, preferred_element_type=F32))
+        pm[0, :, k * 128:(k + 1) * 128] = hi
+        pm[1, :, k * 128:(k + 1) * 128] = lo
 
     for c in copies:
         c.wait()
@@ -404,13 +384,18 @@
     for l in (2, 3, 4):
         lx[DROW[l] - 19] = mu * lx[DROW[l] - 19]
 
-    tt = []
-    for rho in range(2):
-        c = cf[pl.ds(lat + rho, 1), :]
-        tt.append(sum(cbuf[a] * c[:, a * 128:(a + 1) * 128] for a in range(8)))
-    u2 = mm(jnp.concatenate(tt, axis=1), "Sel", 0)
-    s_o[0:half, :] = u2[:, 0:128]
-    s_o[half:LP, :] = u2[:, 128:256]
+    hi, lo = split(lx[SROW[4] - 19])
+    fold = dot(hi, pm[0]) + dot(lo, pm[0]) + dot(hi, pm[1])
+    for k in range(NLON_D):
+        acc = jnp.zeros((FOLD, 128), F32)
+        for g in range(LP // FOLD):
+            acc = jnp.where((lane >= g * WIDE) & (lane < (g + 1) * WIDE),
+                            fold[g * FOLD:(g + 1) * FOLD, k * 128:(k + 1) * 128], acc)
+        sf[k] = acc
+    for k in range(1, NLON_D):
+        go(remote(sf.at[k], mf.at[k], at_lon(k)))
+    coarse = copies[:]
+    copies.clear()
 
     groups = {1: (0, 19), 2: (19, 30), 3: (30, 37), 4: (37, 42)}
 
@@ -420,8 +405,8 @@
             return rw[...].reshape(19 * LP, 128)
         return lx[lo - 19:hi - 19].reshape((hi - lo) * LP, 256)
 
-    s_l[...] = s_o[...]
-    s_r[...] = s_o[...]
+    s_l[...] = jnp.zeros((LP, 128), F32)
+    s_r[...] = jnp.zeros((LP, 128), F32)
     for l in (1, 2, 3, 4):
         lo, hi = groups[l]
         tmsg[0:hi - lo] = mm(operand(l), "G", l).reshape(hi - lo, LP, 256)
@@ -433,16 +418,26 @@
             dst[...] = v
     go(remote(s_l, m_l, at_lon(1)))
     go(remote(s_r, m_r, at_lon(-1)))
-    go(remote(s_o, m_o, at_lon(2)))
+
+    for c in coarse:
+        c.wait()
+    row = sf[0] + mf[1] + mf[2] + mf[3]
+    sf[0] = row
+    cbuf[lat] = row
+    round2 = copies[:]
+    copies.clear()
+    for k in range(1, NLAT_D):
+        go(remote(sf.at[0], cbuf.at[lat], at_lat(k)))
+    coarse = copies[:]
+    copies.clear()
 
     o1[...] = mm(operand(1), "W", 1).reshape(19, LP, 256)
     for l in (2, 3, 4):
         lo, hi = groups[l]
         o2[lo - 19:hi - 19] = mm(operand(l), "W", l).reshape(hi - lo, LP, 128)
 
-    for c in copies:
+    for c in round2:
         c.wait()
-    copies.clear()
 
     rl_hi, rl_lo = split(m_l[...])
     rr_hi, rr_lo = split(m_r[...])
@@ -487,10 +482,14 @@
             else:
                 bd[j] = jnp.where(low, 0.0, vmul((3 * l - 3,), t)[0])
 
-    uhi, ulo = split(jnp.concatenate([s_o[...], m_l[...], m_r[...], m_o[...]], axis=1))
-    c = dot(uhi, qm[0]) + dot(ulo, qm[0]) + dot(uhi, qm[1])
+    for c in coarse:
+        c.wait()
     for rho in range(2):
-        v = vmul((BANDS - 1,), c[:, rho * 128:(rho + 1) * 128])[0]
+        w = latf[pl.ds(jnp.minimum(lat + rho, NLAT_D - 1), 1), :]
+        t = sum(cbuf[a] * w[:, a:a + 1] for a in range(NLAT_D))
+        parts = [t if g == 0 else pltpu.roll(t, 128 - WIDE * g, 1) for g in range(LP // FOLD)]
+        c = jnp.where(lane < WIDE, jnp.concatenate(parts, axis=0), 0.0)
+        v = vmul((BANDS - 1,), c)[0]
         sm[rho] = v * mw if rho else v
 
     for l in (4, 3, 2):
@@ -520,39 +519,48 @@
         go(remote(ys.at[pl.ds(4 * q, 4)], prev.at[pl.ds(4 * q, 4)], at_tm(1)))
     for r in range(ROWS):
         inc[pl.ds(r, LEV, stride=ROWS), :] = ys[r, 0:LEV, :]
+    out = pltpu.make_async_copy(inc, inc_hbm, load.at[6])
+    out.start()
     first = (tm > 0).astype(F32)
     for q in range(4):
         copies[q].wait()
         for r in range(4 * q, 4 * q + 4):
             jump[pl.ds(r, LEV, stride=ROWS), :] = ys[r, 0:LEV, :] - first * prev[r, 0:LEV, :]
+    out2 = pltpu.make_async_copy(jump, jump_hbm, load.at[7])
+    out2.start()
+    out.wait()
+    out2.wait()
 
 
 def body(forcing, vertical, lat_factor, lon_factor):
     x = forcing.reshape(LEV * ROWS, COLS)
     tile = (LP, 128)
-    vm = pl.BlockSpec(memory_space=pltpu.VMEM)
+    anywhere = pl.BlockSpec(memory_space=pl.ANY)
     S = pltpu.VMEM
+    flat = (LEV * ROWS, COLS)
     scratch = [
+        S(flat, F32), S((BANDS, LEV, LEV), F32), S((8, 8), F32), S((32, 32), F32), S(CB.shape, BF), S(EXT.shape, F32),
+        S(flat, F32), S(flat, F32),
         S((ROWS,) + tile, F32), S((39,) + tile, F32), S((19,) + tile, F32), S((23, LP, 256), F32),
-        S((3,) + tile, F32), S((2,) + tile, F32), S((2,) + tile, F32), S((LP // 2, 128), F32),
+        S((3,) + tile, F32), S((2,) + tile, F32), S((2,) + tile, F32),
         S((2,) + tile, F32), S(tile, F32), S(tile, F32), S(tile, F32), S(tile, F32), S(tile, F32),
-        S((8, LP // 2, 128), F32),
-        S((BANDS, 2 * LP, 256), BF), S((LP, 256), F32), S((16, 1024), F32), S((2, 512, 256), BF),
+        S((BANDS, 2 * LP, 256), BF), S((LP, 256), F32), S((2, 256, 512), BF),
         S((19, LP, 256), F32), S((23,) + tile, F32), S((19, LP, 256), F32),
-        S(tile, F32), S(tile, F32), S(tile, F32), S(tile, F32), S(tile, F32), S(tile, F32),
+        S(tile, F32), S(tile, F32), S(tile, F32), S(tile, F32),
+        S((4, FOLD, 128), F32), S((4, FOLD, 128), F32), S((8, FOLD, 128), F32),
         S((52,) + tile, F32), S((9,) + tile, F32), S((ROWS,) + tile, F32), S((ROWS,) + tile, F32),
-        pltpu.SemaphoreType.DMA((24,)), pltpu.SemaphoreType.DMA((24,)),
+        pltpu.SemaphoreType.DMA((24,)), pltpu.SemaphoreType.DMA((24,)), pltpu.SemaphoreType.DMA((8,)),
     ]
     out = jax.ShapeDtypeStruct((LEV * ROWS, COLS), F32)
     inc, jump = pl.pallas_call(
         kernel,
         out_shape=(out, out),
-        in_specs=[vm] * 7,
-        out_specs=(vm, vm),
+        in_specs=[anywhere] * 6,
+        out_specs=(anywhere, anywhere),
         scratch_shapes=scratch,
         compiler_params=pltpu.CompilerParams(
             collective_id=0, has_side_effects=True, vmem_limit_bytes=56 * 1024 * 1024),
-    )(x, vertical, lat_factor, lon_factor, jnp.asarray(CB), jnp.asarray(EXT), jnp.asarray(EXPAND))
+    )(x, vertical, lat_factor, lon_factor, jnp.asarray(CB), jnp.asarray(EXT))
     shape = (1, LEV, ROWS, COLS)
     return inc.reshape(shape), jump.reshape(shape)
 

time: 57.3 us -> 52.3 us (0.913); the launches traced: 56.2 us -> 52.1 us
  Pallas kernels: 52.1 us -> 48 us
    pallas_call x1, Pallas kernels: 52.1 us -> 48 us  [body(): pl.pallas_call(kernel, out_shape=(out, out), in_specs=[anywhere] * 6, out...]
where the time goes in v2:
time: 52.3 us; the launch traced here: 52.1 us
  Pallas kernels  48 us (92%)
  local copies, waits for them, and re-layouts  3.41 us (7%)
  between operations  0.65 us (1%)
    pallas_call x1, Pallas kernels, body(): pl.pallas_call(kernel, out_shape=(out, out), in_specs=[anywhere] * 6, out...  48 us
    unnamed x4, local copies, waits for them, and re-layouts  3.41 us

profile of v2, /device:TPU:2, one launch (start us, length us, event | category | flops | bytes accessed | tf_op | source)
XLA Modules:
  0.0 52.1 jit_solution(9136035411287031011)
XLA Ops:
  0.6 48.0 %shard_map.77 = (f32[2192,128]{1,0:T(8,128)}, f32[2192,128]{1,0:T(8,128)}) custom-call(f32[2192,128]{1,0:T(8,128)} %bitcast.3, f32[13,137,137]{2,1,0:T(8,128)} %vert_hbm.1, f32[8,8]{1,0:T(8,128)} %latf_hbm.1, f32[32,32]{1,0:T(8,128)} %lonf_hbm.1, bf16[4864,256]{1,0:T(8,128)(2,1)} %constant.4.clone.cb_hbm, f32[48,128]{1,0:T(8,128)} %constant.5.clone.ext_hbm), custom_call_target="tpu_custom_call" | custom-call | tf_op jit(solution)/shard_map/pallas_call | solution.py:555
  48.7 0.0 copy-start
  48.7 2.4 %copy.10 = f32[1,137,16,128]{3,2,1,0:T(8,128)} copy(f32[1,137,16,128]{3,2,1,0:T(8,128)} %bitcast.5) | data formatting | bytes 2244608
  51.1 0.0 copy-done
  51.1 1.0 %copy.11 = f32[1,137,16,128]{3,2,1,0:T(8,128)} copy(f32[1,137,16,128]{3,2,1,0:T(8,128)S(1)} %bitcast.4) | data formatting | bytes 2244608
Async XLA Ops:
  48.7 2.4 %copy-start = (f32[2192,128]{1,0:T(8,128)S(1)}, f32[2192,128]{1,0:T(8,128)}, u32[]{:S(2)}) copy-start(f32[2192,128]{1,0:T(8,128)} %get-tuple-element.5) | copy-start | bytes 3366916

commit v3 on v2

--- a/solution.py
+++ b/solution.py
@@ -229,8 +229,8 @@
 def kernel(x_hbm, vert_hbm, latf_hbm, lonf_hbm, cb_hbm, ext_hbm, inc_hbm, jump_hbm,
            x, vert, latf, lonf, cb, ext_c, inc, jump,
            xs, so, rw, lx, up, dn, p2, r_w, r_u, r_pw, r_pu, r_p2u, r_p2w,
-           vst, vtmp, pm, o1, o2, tmsg, s_l, s_r, m_l, m_r, sf, mf, cbuf,
-           bd, sm, ys, prev, send, recv, load):
+           vst, vtmp, pm, o1, o2, tl, tmsg, s_l, s_r, m_l, m_r, sf, mf, cbuf,
+           bd, sm, pk, pkp, ys, yz, prev, send, recv, load):
     tm, lat, lon = lax.axis_index("tm"), lax.axis_index("lat"), lax.axis_index("lon")
     mu = (lat > 0).astype(F32)
     mw = (lat < NLAT_D - 1).astype(F32)
@@ -321,14 +321,50 @@
     dn[1] = mm(so[30], "Sm", 2) + mm(so[34], "Sm", 3) + d4
     p2[0] = mm(so[38], "Sm", 4)
     p2[1] = mm(so[36], "Sm", 4)
+    for i in range(1, 7):
+        rw[10 + i] = xs[2 * i] + 0.25 * (rw[i] + rw[i + 1])
+
+    lane = lax.broadcasted_iota(jnp.int32, (1, 128), 1)
+    inner, outer = (1, 8, 11, 17), (0, 1, 8, 11, 17, 19)
+
+    def spans(marks):
+        return list(zip(marks[0::2], marks[1::2]))
+
+    def operand(lo, hi):
+        if hi <= 19:
+            return rw[lo:hi].reshape((hi - lo) * LP, 128)
+        return lx[lo - 19:hi - 19].reshape((hi - lo) * LP, 256)
+
+    def message(n, groups):
+        s_l[n] = jnp.zeros((LP, 128), F32)
+        s_r[n] = jnp.zeros((LP, 128), F32)
+        for lo, hi in groups:
+            tmsg[0:hi - lo] = mm(operand(lo, hi), "G", LEVEL_OF[lo][0]).reshape(hi - lo, LP, 256)
+            for dst, table, base in ((s_l, LEFT, 0), (s_r, RIGHT, 128)):
+                v = dst[n]
+                for j in range(lo, hi):
+                    at, names = table[j]
+                    v = jnp.where((lane >= at) & (lane < at + len(names)), tmsg[j - lo, :, base:base + 128], v)
+                dst[n] = v
+
+    def post(n):
+        out = [remote(s_l.at[n], m_l.at[n], at_lon(1)), remote(s_r.at[n], m_r.at[n], at_lon(-1))]
+        for c in out:
+            c.start()
+        return out
+
+    message(0, spans(inner))
     pl.semaphore_wait(barrier, len(partners))
-    go(remote(up.at[pl.ds(0, 2)], r_w, at_lat(-1)))
-    go(remote(dn.at[0], r_u, at_lat(1)))
+    bulk = [remote(up.at[pl.ds(0, 2)], r_w, at_lat(-1)), remote(dn.at[0], r_u, at_lat(1))]
+    for c in bulk:
+        c.start()
+    lon0 = post(0)
     go(remote(up.at[2], r_pw, at_lat(-1)))
     go(remote(dn.at[1], r_pu, at_lat(1)))
     go(remote(p2.at[0], r_p2u, at_lat(2)))
     go(remote(p2.at[1], r_p2w, at_lat(-2)))
-    lane = lax.broadcasted_iota(jnp.int32, (1, 128), 1)
+    packs = copies[:]
+    copies.clear()
 
     for name in ("ext", "lonf", "latf", "vert"):
         loads[name].wait()
@@ -351,17 +387,104 @@
         pm[0, :, k * 128:(k + 1) * 128] = hi
         pm[1, :, k * 128:(k + 1) * 128] = lo
 
-    for c in copies:
+    low = lane < 64
+    z1 = const(("Z", 1, "hi"))
+    lane2 = lax.broadcasted_iota(jnp.int32, (1, 256), 1)
+
+    def received(j, rhi, rlo):
+        (al, nl), (ar, nr) = LEFT[j], RIGHT[j]
+        keep = ((lane2 >= al) & (lane2 < al + len(nl))) | ((lane2 >= 128 + ar) & (lane2 < 128 + ar + len(nr)))
+        keep = keep.astype(F32)
+        return jnp.concatenate([(rhi * keep).astype(BF), (rlo * keep).astype(BF)], axis=0)
+
+    def vmul(ks, t):
+        hi, lo = split(t)
+        both = jnp.concatenate([hi, lo], axis=1)
+        outs = []
+        for k in ks:
+            p = dot(vst[k][:, 0:LP], both)
+            outs.append(p[0:LP, 0:128] + p[0:LP, 128:256] + p[LP:2 * LP, 0:128])
+        return outs
+
+    def arrived(n):
+        rl_hi, rl_lo = split(m_l[n])
+        rr_hi, rr_lo = split(m_r[n])
+        return (jnp.concatenate([rl_hi, rr_hi], axis=1).astype(F32),
+                jnp.concatenate([rl_lo, rr_lo], axis=1).astype(F32))
+
+    def own_part(lo, hi):
+        if lo < 10:
+            o1[lo:hi] = mm(operand(lo, hi), "W", 1).reshape(hi - lo, LP, 256)
+        else:
+            h, l = split(operand(lo, hi))
+            w = const(("W", 1, "hi"))[:, 128:256]
+            o1[lo:hi, :, 128:256] = (dot(h, w) + dot(l, w)).reshape(hi - lo, LP, 128)
+
+    def bands1(js, halves):
+        for j in js:
+            if j < 10:
+                p = dot(received(j, *halves), z1)
+                t = o1[j] + p[0:LP] + p[LP:2 * LP]
+                bd[42 + j] = vmul((1,), t[:, 0:128])[0]
+                bd[j] = vmul((2,), t[:, 128:256])[0]
+            else:
+                p = dot(received(j, *halves), z1[:, 128:256])
+                bd[j] = vmul((0,), o1[j, :, 128:256] + p[0:LP] + p[LP:2 * LP])[0]
+
+    def even(i):
+        tl[2 * i, :, 0:128] = -0.25 * (bd[42 + i] + bd[43 + i])
+        tl[2 * i, :, 128:256] = bd[10 + i] - 0.25 * (bd[i] + bd[i + 1])
+
+    def odd(i):
+        tl[2 * i + 1, :, 0:128] = bd[43 + i] + 0.5 * (tl[2 * i, :, 0:128] + tl[2 * i + 2, :, 0:128])
+        tl[2 * i + 1, :, 128:256] = bd[1 + i] + 0.5 * (tl[2 * i, :, 128:256] + tl[2 * i + 2, :, 128:256])
+
+    def level1(lo, hi):
+        ys[lo:hi] = mm(tl[lo:hi].reshape((hi - lo) * LP, 256), "T", 1).reshape(hi - lo, LP, 128)
+
+    def to_next(src, dst):
+        c = remote(src, dst, at_tm(1))
+
+        @pl.when(tm < 3)
+        def _():
+            c.start()
+
+        return c
+
+    @pl.when(tm == 0)
+    def _():
+        prev[...] = jnp.zeros((ROWS, LP, 128), F32)
+        pkp[...] = jnp.zeros((5, LP, 128), F32)
+
+    for lo, hi in spans(inner):
+        own_part(lo, hi)
+    for c in lon0:
         c.wait()
-    copies.clear()
-
+    bands1(list(range(1, 8)) + list(range(11, 17)), arrived(0))
+    for i in range(1, 7):
+        even(i)
+    for i in range(1, 6):
+        odd(i)
+    level1(2, 13)
+    shift = [to_next(ys.at[pl.ds(2, 11)], prev.at[pl.ds(2, 11)])]
+
+    for c in bulk:
+        c.wait()
     x16 = lambda: mw * r_w[0]
     rw[0] = mu * r_u[...] - 0.5 * xs[0]
     rw[8] = dn[0] - 0.5 * x16()
     rw[9] = mw * r_w[1]
-    for i in range(8):
-        rw[10 + i] = xs[2 * i] + 0.25 * (rw[i] + rw[i + 1])
+    rw[10] = xs[0] + 0.25 * (rw[0] + rw[1])
+    rw[17] = xs[14] + 0.25 * (rw[7] + rw[8])
     rw[18] = x16() + (0.25 * mw) * (rw[8] + rw[9])
+    rw[0] = mu * rw[0]
+    message(1, spans(outer))
+    lon1 = post(1)
+    for lo, hi in spans(outer):
+        own_part(lo, hi)
+
+    for c in packs:
+        c.wait()
     raw = lambda j: rw[j] if j < 19 else lx[j - 19, :, 0:128]
     for l in (2, 3, 4):
         m, a, d, b = MLAT[l], SROW[l - 1], DROW[l], SROW[l]
@@ -380,7 +503,6 @@
         if kind == "S" and i == MLAT[l]:
             cu, cw = cu * mw, cw * mw
         lx[j - 19, :, 128:256] = r_pu[...] * cu + r_pw[...] * cw
-    rw[0] = mu * rw[0]
     for l in (2, 3, 4):
         lx[DROW[l] - 19] = mu * lx[DROW[l] - 19]
 
@@ -397,84 +519,41 @@
     coarse = copies[:]
     copies.clear()
 
-    groups = {1: (0, 19), 2: (19, 30), 3: (30, 37), 4: (37, 42)}
-
-    def operand(l):
-        lo, hi = groups[l]
-        if l == 1:
-            return rw[...].reshape(19 * LP, 128)
-        return lx[lo - 19:hi - 19].reshape((hi - lo) * LP, 256)
-
-    s_l[...] = jnp.zeros((LP, 128), F32)
-    s_r[...] = jnp.zeros((LP, 128), F32)
-    for l in (1, 2, 3, 4):
-        lo, hi = groups[l]
-        tmsg[0:hi - lo] = mm(operand(l), "G", l).reshape(hi - lo, LP, 256)
-        for dst, table, base in ((s_l, LEFT, 0), (s_r, RIGHT, 128)):
-            v = dst[...]
-            for j in range(lo, hi):
-                at, names = table[j]
-                v = jnp.where((lane >= at) & (lane < at + len(names)), tmsg[j - lo, :, base:base + 128], v)
-            dst[...] = v
-    go(remote(s_l, m_l, at_lon(1)))
-    go(remote(s_r, m_r, at_lon(-1)))
+    message(2, ((19, 30), (30, 37), (37, 42)))
+    lon2 = post(2)
 
     for c in coarse:
         c.wait()
     row = sf[0] + mf[1] + mf[2] + mf[3]
     sf[0] = row
     cbuf[lat] = row
-    round2 = copies[:]
-    copies.clear()
     for k in range(1, NLAT_D):
         go(remote(sf.at[0], cbuf.at[lat], at_lat(k)))
     coarse = copies[:]
     copies.clear()
 
-    o1[...] = mm(operand(1), "W", 1).reshape(19, LP, 256)
+    for c in lon1:
+        c.wait()
+    bands1((0, 8, 9, 10, 17, 18), arrived(1))
+    for i in (0, 7, 8):
+        even(i)
+    for i in (0, 6, 7):
+        odd(i)
+    level1(0, 2)
+    level1(13, 16)
+    shift.append(to_next(ys.at[pl.ds(0, 2)], prev.at[pl.ds(0, 2)]))
+    shift.append(to_next(ys.at[pl.ds(13, 3)], prev.at[pl.ds(13, 3)]))
+    groups = {2: (19, 30), 3: (30, 37), 4: (37, 42)}
     for l in (2, 3, 4):
         lo, hi = groups[l]
-        o2[lo - 19:hi - 19] = mm(operand(l), "W", l).reshape(hi - lo, LP, 128)
-
-    for c in round2:
+        o2[lo - 19:hi - 19] = mm(operand(lo, hi), "W", l).reshape(hi - lo, LP, 128)
+    for c in lon2:
         c.wait()
-
-    rl_hi, rl_lo = split(m_l[...])
-    rr_hi, rr_lo = split(m_r[...])
-    rhi = jnp.concatenate([rl_hi, rr_hi], axis=1).astype(F32)
-    rlo = jnp.concatenate([rl_lo, rr_lo], axis=1).astype(F32)
-    lane2 = lax.broadcasted_iota(jnp.int32, (1, 256), 1)
-
-    def received(j):
-        (al, nl), (ar, nr) = LEFT[j], RIGHT[j]
-        keep = ((lane2 >= al) & (lane2 < al + len(nl))) | ((lane2 >= 128 + ar) & (lane2 < 128 + ar + len(nr)))
-        keep = keep.astype(F32)
-        return jnp.concatenate([(rhi * keep).astype(BF), (rlo * keep).astype(BF)], axis=0)
-
-    def vmul(ks, t):
-        hi, lo = split(t)
-        both = jnp.concatenate([hi, lo], axis=1)
-        outs = []
-        for k in ks:
-            p = dot(vst[k][:, 0:LP], both)
-            outs.append(p[0:LP, 0:128] + p[0:LP, 128:256] + p[LP:2 * LP, 0:128])
-        return outs
-
-    low = lane < 64
-    z1 = const(("Z", 1, "hi"))
-    for j in range(0, 19):
-        if j < 10:
-            p = dot(received(j), z1)
-            t = o1[j] + p[0:LP] + p[LP:2 * LP]
-            bd[42 + j] = vmul((1,), t[:, 0:128])[0]
-            bd[j] = vmul((2,), t[:, 128:256])[0]
-        else:
-            p = dot(received(j), z1[:, 128:256])
-            bd[j] = vmul((0,), o1[j, :, 128:256] + p[0:LP] + p[LP:2 * LP])[0]
-    for l in (2, 3, 4):
+    halves = arrived(2)
+    for l in (4, 3, 2):
         z = const(("Z", l, "hi"))
         for j in range(*groups[l]):
-            p = dot(received(j), z)
+            p = dot(received(j, *halves), z)
             t = o2[j - 19] + p[0:LP] + p[LP:2 * LP]
             if LEVEL_OF[j][1] == "D":
                 a, b = vmul((3 * l - 2, 3 * l - 1), t)
@@ -507,27 +586,49 @@
         out = mm(tmsg[0:n, :, 0:128].reshape(n * LP, 128), "T", l).reshape(n, LP, 128)
         sm[0:n] = out
         sm[2 * m] = mw * sm[2 * m]
-    for i in range(9):
-        tmsg[2 * i, :, 0:128] = sm[i] - 0.25 * (bd[42 + i] + bd[43 + i])
-        tmsg[2 * i, :, 128:256] = bd[10 + i] - 0.25 * (bd[i] + bd[i + 1])
-    for i in range(8):
-        tmsg[2 * i + 1, :, 0:128] = bd[43 + i] + 0.5 * (tmsg[2 * i, :, 0:128] + tmsg[2 * i + 2, :, 0:128])
-        tmsg[2 * i + 1, :, 128:256] = bd[1 + i] + 0.5 * (tmsg[2 * i, :, 128:256] + tmsg[2 * i + 2, :, 128:256])
-    for q in range(4):
-        y = mm(tmsg[4 * q:4 * q + 4].reshape(4 * LP, 256), "T", 1).reshape(4, LP, 128)
-        ys[4 * q:4 * q + 4] = y
-        go(remote(ys.at[pl.ds(4 * q, 4)], prev.at[pl.ds(4 * q, 4)], at_tm(1)))
+
+    last = sm[8]
+    for k in range(9):
+        last = jnp.where(lane == 64 + k, sm[k] if k == 0 else pltpu.roll(sm[k], k, 1), last)
+    for k in range(4):
+        pk[k] = jnp.where(low, sm[k], pltpu.roll(sm[k + 4], 64, 1))
+    pk[4] = last
+    shift.append(to_next(pk, pkp))
+
+    def lifted(rows):
+        w = const(("T", 1, "hi"))[0:128]
+        for i in range(8):
+            tmsg[2 * i, :, 0:128] = rows[i]
+            tmsg[2 * i + 1, :, 0:128] = 0.5 * (rows[i] + rows[i + 1])
+        h, l = split(tmsg[0:16, :, 0:128].reshape(16 * LP, 128))
+        return (dot(h, w) + dot(l, w)).reshape(ROWS, LP, 128)
+
+    yz[...] = ys[...] + lifted(sm)
     for r in range(ROWS):
-        inc[pl.ds(r, LEV, stride=ROWS), :] = ys[r, 0:LEV, :]
+        inc[pl.ds(r, LEV, stride=ROWS), :] = yz[r, 0:LEV, :]
     out = pltpu.make_async_copy(inc, inc_hbm, load.at[6])
     out.start()
-    first = (tm > 0).astype(F32)
-    for q in range(4):
-        copies[q].wait()
-        for r in range(4 * q, 4 * q + 4):
-            jump[pl.ds(r, LEV, stride=ROWS), :] = ys[r, 0:LEV, :] - first * prev[r, 0:LEV, :]
+
+    def settle(cs):
+        for c in cs:
+            pl.when(tm > 0)(c.wait_recv)
+
+    settle(shift[:3])
+    yz[...] = yz[...] - prev[...]
+    settle(shift[3:])
+    for k in range(9):
+        part = pkp[k % 4] if k < 8 else pkp[4]
+        if 4 <= k < 8:
+            part = pltpu.roll(part, 64, 1)
+        end = pkp[4] if k == 0 else pltpu.roll(pkp[4], 128 - k, 1)
+        sm[k] = jnp.where(lane == 64, end, part)
+    yz[...] = yz[...] - lifted(sm)
+    for r in range(ROWS):
+        jump[pl.ds(r, LEV, stride=ROWS), :] = yz[r, 0:LEV, :]
     out2 = pltpu.make_async_copy(jump, jump_hbm, load.at[7])
     out2.start()
+    for c in shift:
+        pl.when(tm < 3)(c.wait_send)
     out.wait()
     out2.wait()
 
@@ -545,11 +646,12 @@
         S((3,) + tile, F32), S((2,) + tile, F32), S((2,) + tile, F32),
         S((2,) + tile, F32), S(tile, F32), S(tile, F32), S(tile, F32), S(tile, F32), S(tile, F32),
         S((BANDS, 2 * LP, 256), BF), S((LP, 256), F32), S((2, 256, 512), BF),
-        S((19, LP, 256), F32), S((23,) + tile, F32), S((19, LP, 256), F32),
-        S(tile, F32), S(tile, F32), S(tile, F32), S(tile, F32),
+        S((19, LP, 256), F32), S((23,) + tile, F32), S((17, LP, 256), F32), S((19, LP, 256), F32),
+        S((3,) + tile, F32), S((3,) + tile, F32), S((3,) + tile, F32), S((3,) + tile, F32),
         S((4, FOLD, 128), F32), S((4, FOLD, 128), F32), S((8, FOLD, 128), F32),
-        S((52,) + tile, F32), S((9,) + tile, F32), S((ROWS,) + tile, F32), S((ROWS,) + tile, F32),
-        pltpu.SemaphoreType.DMA((24,)), pltpu.SemaphoreType.DMA((24,)), pltpu.SemaphoreType.DMA((8,)),
+        S((52,) + tile, F32), S((9,) + tile, F32), S((5,) + tile, F32), S((5,) + tile, F32),
+        S((ROWS,) + tile, F32), S((ROWS,) + tile, F32), S((ROWS,) + tile, F32),
+        pltpu.SemaphoreType.DMA((32,)), pltpu.SemaphoreType.DMA((32,)), pltpu.SemaphoreType.DMA((8,)),
     ]
     out = jax.ShapeDtypeStruct((LEV * ROWS, COLS), F32)
     inc, jump = pl.pallas_call(

time: 52.3 us -> 42.7 us (0.82)
  Pallas kernels: 48 us -> 38.5 us
    pallas_call x1, Pallas kernels: 48 us -> 38.5 us  [body(): pl.pallas_call(kernel, out_shape=(out, out), in_specs=[anywhere] * 6, out...]
where the time goes in v3:
time: 42.7 us; the launch traced here: 42.5 us
  Pallas kernels  38.5 us (90%)
  local copies, waits for them, and re-layouts  3.41 us (8%)
  between operations  0.65 us (2%)
    pallas_call x1, Pallas kernels, body(): pl.pallas_call(kernel, out_shape=(out, out), in_specs=[anywhere] * 6, out...  38.5 us
    unnamed x4, local copies, waits for them, and re-layouts  3.41 us

profile of v3, /device:TPU:2, one launch (start us, length us, event | category | flops | bytes accessed | tf_op | source)
XLA Modules:
  0.0 42.5 jit_solution(3100911227477605377)
XLA Ops:
  0.6 38.5 %shard_map.77 = (f32[2192,128]{1,0:T(8,128)}, f32[2192,128]{1,0:T(8,128)}) custom-call(f32[2192,128]{1,0:T(8,128)} %bitcast.3, f32[13,137,137]{2,1,0:T(8,128)} %vert_hbm.1, f32[8,8]{1,0:T(8,128)} %latf_hbm.1, f32[32,32]{1,0:T(8,128)} %lonf_hbm.1, bf16[4864,256]{1,0:T(8,128)(2,1)} %constant.4.clone.cb_hbm, f32[48,128]{1,0:T(8,128)} %constant.5.clone.ext_hbm), custom_call_target="tpu_custom_call" | custom-call | tf_op jit(solution)/shard_map/pallas_call | solution.py:657
  39.1 0.0 copy-start
  39.1 2.4 %copy.10 = f32[1,137,16,128]{3,2,1,0:T(8,128)} copy(f32[1,137,16,128]{3,2,1,0:T(8,128)} %bitcast.5) | data formatting | bytes 2244608
  41.5 0.0 copy-done
  41.5 1.0 %copy.11 = f32[1,137,16,128]{3,2,1,0:T(8,128)} copy(f32[1,137,16,128]{3,2,1,0:T(8,128)S(1)} %bitcast.4) | data formatting | bytes 2244608
Async XLA Ops:
  39.1 2.4 %copy-start = (f32[2192,128]{1,0:T(8,128)S(1)}, f32[2192,128]{1,0:T(8,128)}, u32[]{:S(2)}) copy-start(f32[2192,128]{1,0:T(8,128)} %get-tuple-element.5) | copy-start | bytes 3366916

commit v4 on v3

--- a/solution.py
+++ b/solution.py
@@ -44,20 +44,40 @@
     return keep(s), keep(d)
 
 
+INNER, OUTER = ((1, 8), (11, 17)), ((0, 1), (8, 11), (17, 19))
+COARSER = ((19, 30), (30, 37), (37, 42))
+MESSAGES = [[j for lo, hi in part for j in range(lo, hi)] for part in (INNER, OUTER, COARSER)]
+
+
 def message_lanes():
-    left, right = {}, {}
-    nl = nr = 0
-    for j in range(NROWS):
+    left, right, border = {}, {}, []
+    for rows in MESSAGES:
+        n = 0
+        for table in (left, right):
+            for j in rows:
+                l, kind, _ = LEVEL_OF[j]
+                if table is left:
+                    names = ["dm1"] if l == 1 else (["sm", "dm1", "dm"] if kind == "D" else ["dm1", "dm"])
+                else:
+                    names = ["d-1", "d0"] if (l == 1 or kind == "S") else ["s0", "d-1", "d0"]
+                table[j] = (n, names)
+                n += len(names)
+            if table is left:
+                border.append(n)
+        assert n <= 128
+    return left, right, border
+
+
+LEFT, RIGHT, BORDER = message_lanes()
+
+
+def users(n):
+    table = {}
+    for j in MESSAGES[n]:
         l, kind, _ = LEVEL_OF[j]
-        ql = ["dm1"] if l == 1 else (["sm", "dm1", "dm"] if kind == "D" else ["dm1", "dm"])
-        qr = ["d-1", "d0"] if (l == 1 or kind == "S") else ["s0", "d-1", "d0"]
-        left[j], right[j] = (nl, ql), (nr, qr)
-        nl, nr = nl + len(ql), nr + len(qr)
-    assert nl <= 128 and nr <= 128
-    return left, right
-
-
-LEFT, RIGHT = message_lanes()
+        for k in ((3 * l - 2, 3 * l - 1) if kind == "D" else (3 * l - 3,)):
+            table.setdefault(k, []).append(j)
+    return table
 
 
 def lon_tables():
@@ -98,45 +118,55 @@
         for i in range(-1, m + 1):
             w[:, off + i + 1] = fd[l].get(i, zero)
         out["W", l] = w if l == 1 else w[:, :128]
-        g = np.zeros((256, 256))
         pick = {"sm": fs[l].get(m, zero), "dm1": fd[l].get(m - 1, zero), "dm": fd[l].get(m, zero),
                 "s0": fs[l].get(0, zero), "d-1": fd[l].get(-1, zero), "d0": fd[l].get(0, zero)}
-        z = np.zeros((256, 256))
-        for j in range(NROWS):
-            if LEVEL_OF[j][0] != l:
+        for n, rows in enumerate(MESSAGES):
+            rows = [j for j in rows if LEVEL_OF[j][0] == l]
+            if not rows:
                 continue
-            smooth_too = LEVEL_OF[j][1] == "D"
-            for base, (at, names) in ((0, LEFT[j]), (128, RIGHT[j])):
-                for q, name in enumerate(names):
-                    lane = base + at + q
-                    g[:, lane] = pick[name]
-                    row = z[lane]
-                    if base == 0:
+            g = np.zeros((256, 128))
+            for j in rows:
+                for at, names in (LEFT[j], RIGHT[j]):
+                    for q, name in enumerate(names):
+                        g[:, at + q] = pick[name]
+            out["G", n, l] = g
+            for k, js in users(n).items():
+                if k // 3 != l - 1:
+                    continue
+                kind = k % 3
+                z = np.zeros((128, 256 * ((len(js) + 1) // 2)))
+                for p, j in enumerate(js):
+                    smooths = np.zeros((128, 128))
+                    details = np.zeros((128, 128))
+                    at, names = LEFT[j]
+                    for q, name in enumerate(names):
                         if name == "dm1":
-                            row[off + 0] += 1.0
-                            if l == 1 and smooth_too:
-                                row[0] += 0.25
+                            details[at + q, 0] += 1.0
+                            if l == 1:
+                                smooths[at + q, 0] += 0.25
                         if name == "dm":
-                            row[off + 1] += 1.0
-                            if smooth_too:
-                                row[1] += 0.25
+                            details[at + q, 1] += 1.0
+                            smooths[at + q, 1] += 0.25
                         if name == "sm":
-                            row[0] += 1.0
-                    else:
+                            smooths[at + q, 0] += 1.0
+                    at, names = RIGHT[j]
+                    for q, name in enumerate(names):
                         if name == "s0":
-                            row[m] += 1.0
+                            smooths[at + q, m] += 1.0
                         if name == "d-1":
-                            row[off + m] += 1.0
-                            if smooth_too:
-                                row[m - 1] += 0.25
-                                if l == 1:
-                                    row[m] += -1.75
+                            details[at + q, m] += 1.0
+                            smooths[at + q, m - 1] += 0.25
+                            if l == 1:
+                                smooths[at + q, m] += -1.75
                         if name == "d0":
-                            row[off + m + 1] += 1.0
-                            if l == 1 and smooth_too:
-                                row[m] += 0.25
-        out["G", l] = g
-        out["Z", l] = z if l == 1 else z[:, :128]
+                            details[at + q, m + 1] += 1.0
+                            if l == 1:
+                                smooths[at + q, m] += 0.25
+                    if l > 1:
+                        details = np.roll(details, 64, axis=1)
+                    z[:, 128 * p:128 * p + 128] = smooths if kind == 1 else details
+                for c in range(0, z.shape[1], 256):
+                    out["Z", n, k, c // 256] = z[:, c:c + 256]
         n_in = 256 if l == 1 else 128
         eye = np.eye(n_in)
         s = {i: eye[i] for i in range(0, m + 1)}
@@ -176,7 +206,7 @@
         tiles.append(a)
 
     for key, a in CONST.items():
-        if key == ("W", 1) or key == ("G", 1):
+        if key == ("W", 1) or (key[0] == "G" and key[2] == 1):
             a = a[:128]
         hi = a.astype(ml_dtypes.bfloat16)
         lo = (a - hi.astype(np.float64)).astype(ml_dtypes.bfloat16)
@@ -229,7 +259,7 @@
 def kernel(x_hbm, vert_hbm, latf_hbm, lonf_hbm, cb_hbm, ext_hbm, inc_hbm, jump_hbm,
            x, vert, latf, lonf, cb, ext_c, inc, jump,
            xs, so, rw, lx, up, dn, p2, r_w, r_u, r_pw, r_pu, r_p2u, r_p2w,
-           vst, vtmp, pm, o1, o2, tl, tmsg, s_l, s_r, m_l, m_r, sf, mf, cbuf,
+           vst, vtmp, pm, o1, o2, tl, tmsg, sd, m_l, m_r, sf, mf, cbuf,
            bd, sm, pk, pkp, ys, yz, prev, send, recv, load):
     tm, lat, lon = lax.axis_index("tm"), lax.axis_index("lat"), lax.axis_index("lon")
     mu = (lat > 0).astype(F32)
@@ -262,12 +292,12 @@
         at, k, n = CWHERE[key]
         return cb[at:at + k, 0:n]
 
-    def mm(a, name, l):
+    def mm(a, *key):
         hi, lo = split(a)
-        w = const((name, l, "hi"))
+        w = const(key + ("hi",))
         out = dot(hi, w) + dot(lo, w)
-        if (name, l, "lo") in CWHERE:
-            out = out + dot(hi, const((name, l, "lo")))
+        if key + ("lo",) in CWHERE:
+            out = out + dot(hi, const(key + ("lo",)))
         return out
 
     loads["x"].wait()
@@ -325,35 +355,28 @@
         rw[10 + i] = xs[2 * i] + 0.25 * (rw[i] + rw[i + 1])
 
     lane = lax.broadcasted_iota(jnp.int32, (1, 128), 1)
-    inner, outer = (1, 8, 11, 17), (0, 1, 8, 11, 17, 19)
-
-    def spans(marks):
-        return list(zip(marks[0::2], marks[1::2]))
-
     def operand(lo, hi):
         if hi <= 19:
             return rw[lo:hi].reshape((hi - lo) * LP, 128)
         return lx[lo - 19:hi - 19].reshape((hi - lo) * LP, 256)
 
     def message(n, groups):
-        s_l[n] = jnp.zeros((LP, 128), F32)
-        s_r[n] = jnp.zeros((LP, 128), F32)
         for lo, hi in groups:
-            tmsg[0:hi - lo] = mm(operand(lo, hi), "G", LEVEL_OF[lo][0]).reshape(hi - lo, LP, 256)
-            for dst, table, base in ((s_l, LEFT, 0), (s_r, RIGHT, 128)):
-                v = dst[n]
-                for j in range(lo, hi):
-                    at, names = table[j]
-                    v = jnp.where((lane >= at) & (lane < at + len(names)), tmsg[j - lo, :, base:base + 128], v)
-                dst[n] = v
+            tmsg[0:hi - lo, :, 0:128] = mm(operand(lo, hi), "G", n, LEVEL_OF[lo][0]).reshape(hi - lo, LP, 128)
+            v = jnp.zeros((LP, 128), F32) if lo == groups[0][0] else sd[n]
+            for j in range(lo, hi):
+                (a, na), (b, nb) = LEFT[j], RIGHT[j]
+                keep = ((lane >= a) & (lane < a + len(na))) | ((lane >= b) & (lane < b + len(nb)))
+                v = jnp.where(keep, tmsg[j - lo, :, 0:128], v)
+            sd[n] = v
 
     def post(n):
-        out = [remote(s_l.at[n], m_l.at[n], at_lon(1)), remote(s_r.at[n], m_r.at[n], at_lon(-1))]
+        out = [remote(sd.at[n], m_l.at[n], at_lon(1)), remote(sd.at[n], m_r.at[n], at_lon(-1))]
         for c in out:
             c.start()
         return out
 
-    message(0, spans(inner))
+    message(0, INNER)
     pl.semaphore_wait(barrier, len(partners))
     bulk = [remote(up.at[pl.ds(0, 2)], r_w, at_lat(-1)), remote(dn.at[0], r_u, at_lat(1))]
     for c in bulk:
@@ -388,15 +411,6 @@
         pm[1, :, k * 128:(k + 1) * 128] = lo
 
     low = lane < 64
-    z1 = const(("Z", 1, "hi"))
-    lane2 = lax.broadcasted_iota(jnp.int32, (1, 256), 1)
-
-    def received(j, rhi, rlo):
-        (al, nl), (ar, nr) = LEFT[j], RIGHT[j]
-        keep = ((lane2 >= al) & (lane2 < al + len(nl))) | ((lane2 >= 128 + ar) & (lane2 < 128 + ar + len(nr)))
-        keep = keep.astype(F32)
-        return jnp.concatenate([(rhi * keep).astype(BF), (rlo * keep).astype(BF)], axis=0)
-
     def vmul(ks, t):
         hi, lo = split(t)
         both = jnp.concatenate([hi, lo], axis=1)
@@ -406,11 +420,17 @@
             outs.append(p[0:LP, 0:128] + p[0:LP, 128:256] + p[LP:2 * LP, 0:128])
         return outs
 
-    def arrived(n):
-        rl_hi, rl_lo = split(m_l[n])
-        rr_hi, rr_lo = split(m_r[n])
-        return (jnp.concatenate([rl_hi, rr_hi], axis=1).astype(F32),
-                jnp.concatenate([rl_lo, rr_lo], axis=1).astype(F32))
+    def settle(n):
+        got = jnp.where(lane < BORDER[n], m_l[n], m_r[n])
+        for k, js in users(n).items():
+            hi, lo = split(vmul((k,), got)[0])
+            both = jnp.concatenate([hi, lo], axis=1)
+            for c in range((len(js) + 1) // 2):
+                z = const(("Z", n, k, c, "hi"))
+                p = dot(both, jnp.concatenate([z, z], axis=0))
+                for h, j in enumerate(js[2 * c:2 * c + 2]):
+                    at = j + 42 if k == 1 else j
+                    bd[at] = bd[at] + p[:, 128 * h:128 * h + 128]
 
     def own_part(lo, hi):
         if lo < 10:
@@ -420,16 +440,23 @@
             w = const(("W", 1, "hi"))[:, 128:256]
             o1[lo:hi, :, 128:256] = (dot(h, w) + dot(l, w)).reshape(hi - lo, LP, 128)
 
-    def bands1(js, halves):
+    def bands1(js):
         for j in js:
             if j < 10:
-                p = dot(received(j, *halves), z1)
-                t = o1[j] + p[0:LP] + p[LP:2 * LP]
-                bd[42 + j] = vmul((1,), t[:, 0:128])[0]
-                bd[j] = vmul((2,), t[:, 128:256])[0]
+                bd[42 + j] = vmul((1,), o1[j, :, 0:128])[0]
+                bd[j] = vmul((2,), o1[j, :, 128:256])[0]
             else:
-                p = dot(received(j, *halves), z1[:, 128:256])
-                bd[j] = vmul((0,), o1[j, :, 128:256] + p[0:LP] + p[LP:2 * LP])[0]
+                bd[j] = vmul((0,), o1[j, :, 128:256])[0]
+
+    def bands(l):
+        lo, hi = COARSER[l - 2]
+        o2[lo - 19:hi - 19] = mm(operand(lo, hi), "W", l).reshape(hi - lo, LP, 128)
+        for j in range(lo, hi):
+            if LEVEL_OF[j][1] == "D":
+                a, b = vmul((3 * l - 2, 3 * l - 1), o2[j - 19])
+                bd[j] = jnp.where(low, a, b)
+            else:
+                bd[j] = jnp.where(low, 0.0, vmul((3 * l - 3,), o2[j - 19])[0])
 
     def even(i):
         tl[2 * i, :, 0:128] = -0.25 * (bd[42 + i] + bd[43 + i])
@@ -456,11 +483,12 @@
         prev[...] = jnp.zeros((ROWS, LP, 128), F32)
         pkp[...] = jnp.zeros((5, LP, 128), F32)
 
-    for lo, hi in spans(inner):
+    for lo, hi in INNER:
         own_part(lo, hi)
+    bands1(MESSAGES[0])
     for c in lon0:
         c.wait()
-    bands1(list(range(1, 8)) + list(range(11, 17)), arrived(0))
+    settle(0)
     for i in range(1, 7):
         even(i)
     for i in range(1, 6):
@@ -478,10 +506,11 @@
     rw[17] = xs[14] + 0.25 * (rw[7] + rw[8])
     rw[18] = x16() + (0.25 * mw) * (rw[8] + rw[9])
     rw[0] = mu * rw[0]
-    message(1, spans(outer))
+    message(1, OUTER)
     lon1 = post(1)
-    for lo, hi in spans(outer):
+    for lo, hi in OUTER:
         own_part(lo, hi)
+    bands1(MESSAGES[1])
 
     for c in packs:
         c.wait()
@@ -519,8 +548,10 @@
     coarse = copies[:]
     copies.clear()
 
-    message(2, ((19, 30), (30, 37), (37, 42)))
+    message(2, COARSER)
     lon2 = post(2)
+    bands(4)
+    bands(3)
 
     for c in coarse:
         c.wait()
@@ -534,7 +565,7 @@
 
     for c in lon1:
         c.wait()
-    bands1((0, 8, 9, 10, 17, 18), arrived(1))
+    settle(1)
     for i in (0, 7, 8):
         even(i)
     for i in (0, 6, 7):
@@ -543,23 +574,10 @@
     level1(13, 16)
     shift.append(to_next(ys.at[pl.ds(0, 2)], prev.at[pl.ds(0, 2)]))
     shift.append(to_next(ys.at[pl.ds(13, 3)], prev.at[pl.ds(13, 3)]))
-    groups = {2: (19, 30), 3: (30, 37), 4: (37, 42)}
-    for l in (2, 3, 4):
-        lo, hi = groups[l]
-        o2[lo - 19:hi - 19] = mm(operand(lo, hi), "W", l).reshape(hi - lo, LP, 128)
+    bands(2)
     for c in lon2:
         c.wait()
-    halves = arrived(2)
-    for l in (4, 3, 2):
-        z = const(("Z", l, "hi"))
-        for j in range(*groups[l]):
-            p = dot(received(j, *halves), z)
-            t = o2[j - 19] + p[0:LP] + p[LP:2 * LP]
-            if LEVEL_OF[j][1] == "D":
-                a, b = vmul((3 * l - 2, 3 * l - 1), t)
-                bd[j] = jnp.where(low, a, b)
-            else:
-                bd[j] = jnp.where(low, 0.0, vmul((3 * l - 3,), t)[0])
+    settle(2)
 
     for c in coarse:
         c.wait()
@@ -609,13 +627,13 @@
     out = pltpu.make_async_copy(inc, inc_hbm, load.at[6])
     out.start()
 
-    def settle(cs):
+    def land(cs):
         for c in cs:
             pl.when(tm > 0)(c.wait_recv)
 
-    settle(shift[:3])
+    land(shift[:3])
     yz[...] = yz[...] - prev[...]
-    settle(shift[3:])
+    land(shift[3:])
     for k in range(9):
         part = pkp[k % 4] if k < 8 else pkp[4]
         if 4 <= k < 8:
@@ -647,7 +665,7 @@
         S((2,) + tile, F32), S(tile, F32), S(tile, F32), S(tile, F32), S(tile, F32), S(tile, F32),
         S((BANDS, 2 * LP, 256), BF), S((LP, 256), F32), S((2, 256, 512), BF),
         S((19, LP, 256), F32), S((23,) + tile, F32), S((17, LP, 256), F32), S((19, LP, 256), F32),
-        S((3,) + tile, F32), S((3,) + tile, F32), S((3,) + tile, F32), S((3,) + tile, F32),
+        S((3,) + tile, F32), S((3,) + tile, F32), S((3,) + tile, F32),
         S((4, FOLD, 128), F32), S((4, FOLD, 128), F32), S((8, FOLD, 128), F32),
         S((52,) + tile, F32), S((9,) + tile, F32), S((5,) + tile, F32), S((5,) + tile, F32),
         S((ROWS,) + tile, F32), S((ROWS,) + tile, F32), S((ROWS,) + tile, F32),
@@ -663,6 +681,27 @@
         compiler_params=pltpu.CompilerParams(
             collective_id=0, has_side_effects=True, vmem_limit_bytes=56 * 1024 * 1024),
     )(x, vertical, lat_factor, lon_factor, jnp.asarray(CB), jnp.asarray(EXT))
+
+    def settle(a, b, c, d, held, arrive, leave):
+        size = LEV * ROWS // 2
+        moves = []
+        for k in range(2):
+            for h, (src, dst) in enumerate(((a, c), (b, d))):
+                part = pl.ds(k * size, size)
+                moves.append((pltpu.make_async_copy(src.at[part], held.at[h, part], arrive.at[2 * k + h]),
+                              pltpu.make_async_copy(held.at[h, part], dst.at[part], leave.at[2 * k + h])))
+        for m, _ in moves:
+            m.start()
+        for m, o in moves:
+            m.wait()
+            o.start()
+        for _, o in moves:
+            o.wait()
+
+    inc, jump = pl.pallas_call(
+        settle, out_shape=(out, out), in_specs=[anywhere] * 2, out_specs=(anywhere, anywhere),
+        scratch_shapes=[S((2,) + flat, F32), pltpu.SemaphoreType.DMA((4,)), pltpu.SemaphoreType.DMA((4,))],
+    )(inc, jump)
     shape = (1, LEV, ROWS, COLS)
     return inc.reshape(shape), jump.reshape(shape)
 

time: 42.7 us -> 41.5 us (0.972)
  local copies, waits for them, and re-layouts: 3.41 us -> 0 us
  Pallas kernels: 38.5 us -> 40.5 us
    unnamed x4 -> x0, local copies, waits for them, and re-layouts: 3.41 us -> none
    pallas_call x0 -> x1, Pallas kernels: none -> 2.48 us  [body(): pl.pallas_call(settle, out_shape=(out, out), in_specs=[anywhere] * 2, out...]
    pallas_call x1, Pallas kernels: 38.5 us -> 38 us  [body(): pl.pallas_call(kernel, out_shape=(out, out), in_specs=[anywhere] * 6, out...]
where the time goes in v4:
time: 41.5 us; the launch traced here: 41.3 us
  Pallas kernels  40.5 us (98%)
  between operations  0.8 us (2%)
    pallas_call x1, Pallas kernels, body(): pl.pallas_call(kernel, out_shape=(out, out), in_specs=[anywhere] * 6, out...  38 us
    pallas_call x1, Pallas kernels, body(): pl.pallas_call(settle, out_shape=(out, out), in_specs=[anywhere] * 2, out...  2.48 us

profile of v4, /device:TPU:2, one launch (start us, length us, event | category | flops | bytes accessed | tf_op | source)
XLA Modules:
  0.0 41.3 jit_solution(14518074174581649715)
XLA Ops:
  0.6 38.0 %shard_map.77 = (f32[2192,128]{1,0:T(8,128)}, f32[2192,128]{1,0:T(8,128)}) custom-call(f32[2192,128]{1,0:T(8,128)} %bitcast.3, f32[13,137,137]{2,1,0:T(8,128)} %vert_hbm.1, f32[8,8]{1,0:T(8,128)} %latf_hbm.1, f32[32,32]{1,0:T(8,128)} %lonf_hbm.1, bf16[8704,256]{1,0:T(8,128)(2,1)} %constant.4.clone.cb_hbm, f32[48,128]{1,0:T(8,128)} %constant.5.clone.ext_hbm), custom_call_target="tpu_custom_call" | custom-call | tf_op jit(solution)/shard_map/pallas_call | solution.py:675
  38.7 2.5 %shard_map.78 = (f32[2192,128]{1,0:T(8,128)}, f32[2192,128]{1,0:T(8,128)}) custom-call(f32[2192,128]{1,0:T(8,128)} %get-tuple-element.6.a, f32[2192,128]{1,0:T(8,128)} %get-tuple-element.7.b), custom_call_target="tpu_custom_call" | custom-call | tf_op jit(solution)/shard_map/pallas_call | solution.py:701

commit v5 on v4

--- a/solution.py
+++ b/solution.py
@@ -260,7 +260,7 @@
            x, vert, latf, lonf, cb, ext_c, inc, jump,
            xs, so, rw, lx, up, dn, p2, r_w, r_u, r_pw, r_pu, r_p2u, r_p2w,
            vst, vtmp, pm, o1, o2, tl, tmsg, sd, m_l, m_r, sf, mf, cbuf,
-           bd, sm, pk, pkp, ys, yz, prev, send, recv, load):
+           bd, sm, pk, pkp, ys, yz, prev, way, send, recv, load):
     tm, lat, lon = lax.axis_index("tm"), lax.axis_index("lat"), lax.axis_index("lon")
     mu = (lat > 0).astype(F32)
     mw = (lat < NLAT_D - 1).astype(F32)
@@ -273,10 +273,15 @@
     def at_lon(k):
         return (tm, lat, lax.rem(lon + k + NLON_D, NLON_D))
 
+    across = lat + 1 - 2 * lax.rem(lat, 2)
+
+    def at(window, row):
+        return (window, row, lon)
+
     def at_tm(k):
         return (lax.rem(tm + k + 4, 4), lat, lon)
 
-    partners = [at_lat(k) for k in range(1, 8)] + [at_lon(k) for k in range(1, 4)] + [at_tm(1), at_tm(-1)]
+    partners = [at_lat(k) for k in range(1, 8)] + [at_lon(k) for k in range(1, 4)] + [at_tm(1), at_tm(-1), at(lax.rem(tm + 2, 4), across)]
     barrier = pltpu.get_barrier_semaphore()
     for p in partners:
         pl.semaphore_signal(barrier, inc=1, device_id=p, device_id_type=MESH)
@@ -311,7 +316,7 @@
     up[0] = xs[0]
     up[1] = rw[1]
 
-    sems = iter(range(64))
+    sems = iter(range(48))
 
     def remote(src, dst, dev, slot=None):
         k = next(sems)
@@ -494,7 +499,29 @@
     for i in range(1, 6):
         odd(i)
     level1(2, 13)
-    shift = [to_next(ys.at[pl.ds(2, 11)], prev.at[pl.ds(2, 11)])]
+    shift = [to_next(ys.at[pl.ds(2, 7)], prev.at[pl.ds(2, 7)])]
+    straight = remote(ys.at[pl.ds(9, 4)], prev.at[pl.ds(9, 4)], at_tm(1))
+    hops = []
+    for q in range(2):
+        mine, kept, there = ys.at[pl.ds(9 + 2 * q, 2)], way.at[pl.ds(2 * q, 2)], prev.at[pl.ds(9 + 2 * q, 2)]
+        hops.append((remote(mine, kept, at(3, across)), remote(kept, kept, at(0, lat)),
+                     remote(kept, there, at(2, across))))
+
+    @pl.when((tm == 0) | (tm == 2))
+    def _():
+        straight.start()
+
+    @pl.when(tm == 1)
+    def _():
+        for q in range(2):
+            hops[q][0].start()
+
+    def forward(window, hop):
+        @pl.when(tm == window)
+        def _():
+            for q in range(2):
+                hops[q][hop].wait_recv()
+                hops[q][hop + 1].start()
 
     for c in bulk:
         c.wait()
@@ -553,6 +580,8 @@
     bands(4)
     bands(3)
 
+    forward(3, 0)
+
     for c in coarse:
         c.wait()
     row = sf[0] + mf[1] + mf[2] + mf[3]
@@ -578,6 +607,7 @@
     for c in lon2:
         c.wait()
     settle(2)
+    forward(0, 1)
 
     for c in coarse:
         c.wait()
@@ -632,6 +662,13 @@
             pl.when(tm > 0)(c.wait_recv)
 
     land(shift[:3])
+    pl.when((tm == 1) | (tm == 3))(straight.wait_recv)
+
+    @pl.when(tm == 2)
+    def _():
+        for q in range(2):
+            hops[q][2].wait_recv()
+
     yz[...] = yz[...] - prev[...]
     land(shift[3:])
     for k in range(9):
@@ -647,6 +684,13 @@
     out2.start()
     for c in shift:
         pl.when(tm < 3)(c.wait_send)
+    pl.when((tm == 0) | (tm == 2))(straight.wait_send)
+    for window, hop in ((1, 0), (3, 1), (0, 2)):
+        @pl.when(tm == window)
+        def _(hop=hop):
+            for q in range(2):
+                hops[q][hop].wait_send()
+
     out.wait()
     out2.wait()
 
@@ -668,8 +712,8 @@
         S((3,) + tile, F32), S((3,) + tile, F32), S((3,) + tile, F32),
         S((4, FOLD, 128), F32), S((4, FOLD, 128), F32), S((8, FOLD, 128), F32),
         S((52,) + tile, F32), S((9,) + tile, F32), S((5,) + tile, F32), S((5,) + tile, F32),
-        S((ROWS,) + tile, F32), S((ROWS,) + tile, F32), S((ROWS,) + tile, F32),
-        pltpu.SemaphoreType.DMA((32,)), pltpu.SemaphoreType.DMA((32,)), pltpu.SemaphoreType.DMA((8,)),
+        S((ROWS,) + tile, F32), S((ROWS,) + tile, F32), S((ROWS,) + tile, F32), S((4,) + tile, F32),
+        pltpu.SemaphoreType.DMA((48,)), pltpu.SemaphoreType.DMA((48,)), pltpu.SemaphoreType.DMA((8,)),
     ]
     out = jax.ShapeDtypeStruct((LEV * ROWS, COLS), F32)
     inc, jump = pl.pallas_call(

time: 41.5 us -> 41.2 us (level)
  the two profiles are of different devices: /device:TPU:2 before, /device:TPU:6 now
where the time goes in v5:
time: 41.2 us; the launch traced here: 41 us
  Pallas kernels  40.2 us (98%)
  between operations  0.8 us (2%)
    pallas_call x1, Pallas kernels, body(): pl.pallas_call(kernel, out_shape=(out, out), in_specs=[anywhere] * 6, out...  37.7 us
    pallas_call x1, Pallas kernels, body(): pl.pallas_call(settle, out_shape=(out, out), in_specs=[anywhere] * 2, out...  2.48 us

profile of v5, /device:TPU:6, one launch (start us, length us, event | category | flops | bytes accessed | tf_op | source)
XLA Modules:
  0.0 41.0 jit_solution(163484581172873236)
XLA Ops:
  0.6 37.7 %shard_map.77 = (f32[2192,128]{1,0:T(8,128)}, f32[2192,128]{1,0:T(8,128)}) custom-call(f32[2192,128]{1,0:T(8,128)} %bitcast.3, f32[13,137,137]{2,1,0:T(8,128)} %vert_hbm.1, f32[8,8]{1,0:T(8,128)} %latf_hbm.1, f32[32,32]{1,0:T(8,128)} %lonf_hbm.1, bf16[8704,256]{1,0:T(8,128)(2,1)} %constant.4.clone.cb_hbm, f32[48,128]{1,0:T(8,128)} %constant.5.clone.ext_hbm), custom_call_target="tpu_custom_call" | custom-call | tf_op jit(solution)/shard_map/pallas_call | solution.py:719
  38.4 2.5 %shard_map.78 = (f32[2192,128]{1,0:T(8,128)}, f32[2192,128]{1,0:T(8,128)}) custom-call(f32[2192,128]{1,0:T(8,128)} %get-tuple-element.6.a, f32[2192,128]{1,0:T(8,128)} %get-tuple-element.7.b), custom_call_target="tpu_custom_call" | custom-call | tf_op jit(solution)/shard_map/pallas_call | solution.py:745

commit v6 on v5

--- a/solution.py
+++ b/solution.py
@@ -256,11 +256,11 @@
     return jnp.dot(a, b, preferred_element_type=F32)
 
 
-def kernel(x_hbm, vert_hbm, latf_hbm, lonf_hbm, cb_hbm, ext_hbm, inc_hbm, jump_hbm,
-           x, vert, latf, lonf, cb, ext_c, inc, jump,
+def kernel(x_hbm, vert_hbm, latf_hbm, lonf_hbm, cb_hbm, ext_hbm, inc_hbm, yz_hbm, pk_hbm,
+           x, vert, latf, lonf, cb, ext_c, inc,
            xs, so, rw, lx, up, dn, p2, r_w, r_u, r_pw, r_pu, r_p2u, r_p2w,
            vst, vtmp, pm, o1, o2, tl, tmsg, sd, m_l, m_r, sf, mf, cbuf,
-           bd, sm, pk, pkp, ys, yz, prev, way, send, recv, load):
+           bd, sm, smc, pk, fo, fop, ys, yz, prev, way, send, recv, load):
     tm, lat, lon = lax.axis_index("tm"), lax.axis_index("lat"), lax.axis_index("lon")
     mu = (lat > 0).astype(F32)
     mw = (lat < NLAT_D - 1).astype(F32)
@@ -486,7 +486,11 @@
     @pl.when(tm == 0)
     def _():
         prev[...] = jnp.zeros((ROWS, LP, 128), F32)
-        pkp[...] = jnp.zeros((5, LP, 128), F32)
+        fop[...] = jnp.zeros((2, FOLD, 128), F32)
+        pk[...] = jnp.zeros((5, LP, 128), F32)
+        blank = pltpu.make_async_copy(pk, pk_hbm, load.at[7])
+        blank.start()
+        blank.wait()
 
     for lo, hi in INNER:
         own_part(lo, hi)
@@ -499,30 +503,6 @@
     for i in range(1, 6):
         odd(i)
     level1(2, 13)
-    shift = [to_next(ys.at[pl.ds(2, 7)], prev.at[pl.ds(2, 7)])]
-    straight = remote(ys.at[pl.ds(9, 4)], prev.at[pl.ds(9, 4)], at_tm(1))
-    hops = []
-    for q in range(2):
-        mine, kept, there = ys.at[pl.ds(9 + 2 * q, 2)], way.at[pl.ds(2 * q, 2)], prev.at[pl.ds(9 + 2 * q, 2)]
-        hops.append((remote(mine, kept, at(3, across)), remote(kept, kept, at(0, lat)),
-                     remote(kept, there, at(2, across))))
-
-    @pl.when((tm == 0) | (tm == 2))
-    def _():
-        straight.start()
-
-    @pl.when(tm == 1)
-    def _():
-        for q in range(2):
-            hops[q][0].start()
-
-    def forward(window, hop):
-        @pl.when(tm == window)
-        def _():
-            for q in range(2):
-                hops[q][hop].wait_recv()
-                hops[q][hop + 1].start()
-
     for c in bulk:
         c.wait()
     x16 = lambda: mw * r_w[0]
@@ -541,6 +521,31 @@
 
     for c in packs:
         c.wait()
+
+    shift = [to_next(ys.at[pl.ds(2, 7)], prev.at[pl.ds(2, 7)])]
+    straight = remote(ys.at[pl.ds(9, 4)], prev.at[pl.ds(9, 4)], at_tm(1))
+    hops = []
+    for q in range(2):
+        mine, kept, there = ys.at[pl.ds(9 + 2 * q, 2)], way.at[pl.ds(2 * q, 2)], prev.at[pl.ds(9 + 2 * q, 2)]
+        hops.append((remote(mine, kept, at(3, across)), remote(kept, kept, at(0, lat)),
+                     remote(kept, there, at(2, across))))
+
+    @pl.when((tm == 0) | (tm == 2))
+    def _():
+        straight.start()
+
+    @pl.when(tm == 1)
+    def _():
+        for q in range(2):
+            hops[q][0].start()
+
+    def forward(window, hop):
+        @pl.when(tm == window)
+        def _():
+            for q in range(2):
+                hops[q][hop].wait_recv()
+                hops[q][hop + 1].start()
+
     raw = lambda j: rw[j] if j < 19 else lx[j - 19, :, 0:128]
     for l in (2, 3, 4):
         m, a, d, b = MLAT[l], SROW[l - 1], DROW[l], SROW[l]
@@ -607,23 +612,12 @@
     for c in lon2:
         c.wait()
     settle(2)
-    forward(0, 1)
-
-    for c in coarse:
-        c.wait()
-    for rho in range(2):
-        w = latf[pl.ds(jnp.minimum(lat + rho, NLAT_D - 1), 1), :]
-        t = sum(cbuf[a] * w[:, a:a + 1] for a in range(NLAT_D))
-        parts = [t if g == 0 else pltpu.roll(t, 128 - WIDE * g, 1) for g in range(LP // FOLD)]
-        c = jnp.where(lane < WIDE, jnp.concatenate(parts, axis=0), 0.0)
-        v = vmul((BANDS - 1,), c)[0]
-        sm[rho] = v * mw if rho else v
 
     for l in (4, 3, 2):
         m, d, b = MLAT[l], DROW[l], SROW[l]
         for i in range(m + 1):
-            s = bd[b + i] + sm[i]
-            sm[i] = s - 0.25 * (bd[d + i] + bd[d + i + 1])
+            part = bd[b + i] if l == 4 else bd[b + i] + sm[i]
+            sm[i] = part - 0.25 * (bd[d + i] + bd[d + i + 1])
         for i in range(2 * m, -1, -1):
             if i % 2:
                 h = i // 2
@@ -641,7 +635,32 @@
     for k in range(4):
         pk[k] = jnp.where(low, sm[k], pltpu.roll(sm[k + 4], 64, 1))
     pk[4] = last
-    shift.append(to_next(pk, pkp))
+    shift.append(to_next(pk, pk_hbm))
+    forward(0, 1)
+
+    for c in coarse:
+        c.wait()
+    for rho in range(2):
+        w = latf[pl.ds(jnp.minimum(lat + rho, NLAT_D - 1), 1), :]
+        fo[rho] = sum(cbuf[a] * w[:, a:a + 1] for a in range(NLAT_D))
+    shift.append(to_next(fo, fop))
+
+    def climb(folded):
+        for rho in range(2):
+            t = folded[rho]
+            parts = [t if g == 0 else pltpu.roll(t, 128 - WIDE * g, 1) for g in range(LP // FOLD)]
+            c = jnp.where(lane < WIDE, jnp.concatenate(parts, axis=0), 0.0)
+            v = vmul((BANDS - 1,), c)[0]
+            smc[rho] = v * mw if rho else v
+        for l in (4, 3, 2):
+            m = MLAT[l]
+            n = 2 * m + 1
+            for i in range(n):
+                h = i // 2
+                tmsg[i, :, 0:128] = 0.5 * (smc[h] + smc[h + 1]) if i % 2 else smc[h]
+            out = mm(tmsg[0:n, :, 0:128].reshape(n * LP, 128), "T", l).reshape(n, LP, 128)
+            smc[0:n] = out
+            smc[2 * m] = mw * smc[2 * m]
 
     def lifted(rows):
         w = const(("T", 1, "hi"))[0:128]
@@ -651,17 +670,19 @@
         h, l = split(tmsg[0:16, :, 0:128].reshape(16 * LP, 128))
         return (dot(h, w) + dot(l, w)).reshape(ROWS, LP, 128)
 
+    climb(fo)
+    sm[...] = sm[...] + smc[...]
     yz[...] = ys[...] + lifted(sm)
     for r in range(ROWS):
         inc[pl.ds(r, LEV, stride=ROWS), :] = yz[r, 0:LEV, :]
     out = pltpu.make_async_copy(inc, inc_hbm, load.at[6])
     out.start()
 
-    def land(cs):
-        for c in cs:
-            pl.when(tm > 0)(c.wait_recv)
-
-    land(shift[:3])
+    pl.when(tm > 0)(shift[4].wait_recv)
+    climb(fop)
+    yz[...] = yz[...] - lifted(smc)
+    for c in shift[:3]:
+        pl.when(tm > 0)(c.wait_recv)
     pl.when((tm == 1) | (tm == 3))(straight.wait_recv)
 
     @pl.when(tm == 2)
@@ -670,17 +691,7 @@
             hops[q][2].wait_recv()
 
     yz[...] = yz[...] - prev[...]
-    land(shift[3:])
-    for k in range(9):
-        part = pkp[k % 4] if k < 8 else pkp[4]
-        if 4 <= k < 8:
-            part = pltpu.roll(part, 64, 1)
-        end = pkp[4] if k == 0 else pltpu.roll(pkp[4], 128 - k, 1)
-        sm[k] = jnp.where(lane == 64, end, part)
-    yz[...] = yz[...] - lifted(sm)
-    for r in range(ROWS):
-        jump[pl.ds(r, LEV, stride=ROWS), :] = yz[r, 0:LEV, :]
-    out2 = pltpu.make_async_copy(jump, jump_hbm, load.at[7])
+    out2 = pltpu.make_async_copy(yz, yz_hbm, load.at[7])
     out2.start()
     for c in shift:
         pl.when(tm < 3)(c.wait_send)
@@ -693,6 +704,40 @@
 
     out.wait()
     out2.wait()
+    pl.when(tm > 0)(shift[3].wait_recv)
+
+
+def finish(inc_hbm, yz_hbm, pk_hbm, t_hbm, inc_out, jump_out, inc, yz, pk, t, lift, jump, arrive, leave):
+    loads = [pltpu.make_async_copy(src, dst, arrive.at[n])
+             for n, (src, dst) in enumerate(((pk_hbm, pk), (t_hbm, t), (yz_hbm, yz), (inc_hbm, inc)))]
+    for c in loads:
+        c.start()
+    loads[0].wait()
+    lane = lax.broadcasted_iota(jnp.int32, (1, 128), 1)
+    for k in range(9):
+        part = pk[k % 4] if k < 8 else pk[4]
+        if 4 <= k < 8:
+            part = pltpu.roll(part, 64, 1)
+        end = pk[4] if k == 0 else pltpu.roll(pk[4], 128 - k, 1)
+        row = jnp.where(lane == 64, end, part)
+        if k < 8:
+            lift[2 * k] = row
+        if k:
+            lift[2 * k - 1] = 0.5 * (lift[2 * k - 2] + row)
+    loads[1].wait()
+    h, l = split(lift[...].reshape(ROWS * LP, 128))
+    w = t[...]
+    loads[2].wait()
+    lift[...] = yz[...] - (dot(h, w) + dot(l, w)).reshape(ROWS, LP, 128)
+    loads[3].wait()
+    out = pltpu.make_async_copy(inc, inc_out, leave.at[0])
+    out.start()
+    for r in range(ROWS):
+        jump[pl.ds(r, LEV, stride=ROWS), :] = lift[r, 0:LEV, :]
+    out2 = pltpu.make_async_copy(jump, jump_out, leave.at[1])
+    out2.start()
+    out.wait()
+    out2.wait()
 
 
 def body(forcing, vertical, lat_factor, lon_factor):
@@ -703,7 +748,7 @@
     flat = (LEV * ROWS, COLS)
     scratch = [
         S(flat, F32), S((BANDS, LEV, LEV), F32), S((8, 8), F32), S((32, 32), F32), S(CB.shape, BF), S(EXT.shape, F32),
-        S(flat, F32), S(flat, F32),
+        S(flat, F32),
         S((ROWS,) + tile, F32), S((39,) + tile, F32), S((19,) + tile, F32), S((23, LP, 256), F32),
         S((3,) + tile, F32), S((2,) + tile, F32), S((2,) + tile, F32),
         S((2,) + tile, F32), S(tile, F32), S(tile, F32), S(tile, F32), S(tile, F32), S(tile, F32),
@@ -711,41 +756,28 @@
         S((19, LP, 256), F32), S((23,) + tile, F32), S((17, LP, 256), F32), S((19, LP, 256), F32),
         S((3,) + tile, F32), S((3,) + tile, F32), S((3,) + tile, F32),
         S((4, FOLD, 128), F32), S((4, FOLD, 128), F32), S((8, FOLD, 128), F32),
-        S((52,) + tile, F32), S((9,) + tile, F32), S((5,) + tile, F32), S((5,) + tile, F32),
+        S((52,) + tile, F32), S((9,) + tile, F32), S((9,) + tile, F32), S((5,) + tile, F32),
+        S((2, FOLD, 128), F32), S((2, FOLD, 128), F32),
         S((ROWS,) + tile, F32), S((ROWS,) + tile, F32), S((ROWS,) + tile, F32), S((4,) + tile, F32),
         pltpu.SemaphoreType.DMA((48,)), pltpu.SemaphoreType.DMA((48,)), pltpu.SemaphoreType.DMA((8,)),
     ]
     out = jax.ShapeDtypeStruct((LEV * ROWS, COLS), F32)
-    inc, jump = pl.pallas_call(
+    inc, yz, pk = pl.pallas_call(
         kernel,
-        out_shape=(out, out),
+        out_shape=(out, jax.ShapeDtypeStruct((ROWS,) + tile, F32), jax.ShapeDtypeStruct((5,) + tile, F32)),
         in_specs=[anywhere] * 6,
-        out_specs=(anywhere, anywhere),
+        out_specs=(anywhere,) * 3,
         scratch_shapes=scratch,
         compiler_params=pltpu.CompilerParams(
             collective_id=0, has_side_effects=True, vmem_limit_bytes=56 * 1024 * 1024),
     )(x, vertical, lat_factor, lon_factor, jnp.asarray(CB), jnp.asarray(EXT))
-
-    def settle(a, b, c, d, held, arrive, leave):
-        size = LEV * ROWS // 2
-        moves = []
-        for k in range(2):
-            for h, (src, dst) in enumerate(((a, c), (b, d))):
-                part = pl.ds(k * size, size)
-                moves.append((pltpu.make_async_copy(src.at[part], held.at[h, part], arrive.at[2 * k + h]),
-                              pltpu.make_async_copy(held.at[h, part], dst.at[part], leave.at[2 * k + h])))
-        for m, _ in moves:
-            m.start()
-        for m, o in moves:
-            m.wait()
-            o.start()
-        for _, o in moves:
-            o.wait()
-
     inc, jump = pl.pallas_call(
-        settle, out_shape=(out, out), in_specs=[anywhere] * 2, out_specs=(anywhere, anywhere),
-        scratch_shapes=[S((2,) + flat, F32), pltpu.SemaphoreType.DMA((4,)), pltpu.SemaphoreType.DMA((4,))],
-    )(inc, jump)
+        finish, out_shape=(out, out), in_specs=[anywhere] * 4, out_specs=(anywhere, anywhere),
+        scratch_shapes=[S(flat, F32), S((ROWS,) + tile, F32), S((5,) + tile, F32), S((128, 128), BF),
+                        S((ROWS,) + tile, F32), S(flat, F32),
+                        pltpu.SemaphoreType.DMA((4,)), pltpu.SemaphoreType.DMA((2,))],
+        compiler_params=pltpu.CompilerParams(vmem_limit_bytes=40 * 1024 * 1024),
+    )(inc, yz, pk, jnp.asarray(CONST["T", 1][:128].astype(ml_dtypes.bfloat16)))
     shape = (1, LEV, ROWS, COLS)
     return inc.reshape(shape), jump.reshape(shape)
 

time: 41.2 us -> 45.5 us (1.10)
  the two profiles are of different devices: /device:TPU:6 before, /device:TPU:2 now
where the time goes in v6:
time: 45.5 us; the launch traced here: 45.3 us
  Pallas kernels  40.9 us (90%)
  local copies, waits for them, and re-layouts  3.51 us (8%)
  between operations  0.85 us (2%)
    pallas_call x1, Pallas kernels, body(): pl.pallas_call(kernel, out_shape=(out, jax.ShapeDtypeStruct((ROWS,) + til...  37.8 us
    unnamed x8, local copies, waits for them, and re-layouts  3.51 us
    pallas_call x1, Pallas kernels, body(): pl.pallas_call(finish, out_shape=(out, out), in_specs=[anywhere] * 4, out...  3.15 us

profile of v6, /device:TPU:2, one launch (start us, length us, event | category | flops | bytes accessed | tf_op | source)
XLA Modules:
  0.0 45.3 jit_solution(7834209065831886471)
XLA Ops:
  0.6 0.0 copy-start.3
  0.6 37.8 %shard_map.86 = (f32[2192,128]{1,0:T(8,128)}, f32[16,144,128]{2,1,0:T(8,128)}, f32[5,144,128]{2,1,0:T(8,128)}) custom-call(f32[2192,128]{1,0:T(8,128)} %bitcast.3, f32[13,137,137]{2,1,0:T(8,128)} %vert_hbm.1, f32[8,8]{1,0:T(8,128)} %latf_hbm.1, f32[32,32]{1,0:T(8,128)} %lonf_hbm.1, bf16[8704,256]{1,0:T(8,128)(2,1)} %constant.6.clone.cb_hbm, ...), custom_call_target="tpu_custom_call" | custom-call | tf_op jit(solution)/shard_map/pallas_call | solution.py:765
  38.4 0.0 copy-done.3
  38.4 0.0 copy-start
  38.5 1.3 %copy-done = f32[16,144,128]{2,1,0:T(8,128)S(1)} copy-done((f32[16,144,128]{2,1,0:T(8,128)S(1)}, f32[16,144,128]{2,1,0:T(8,128)}, u32[]{:S(2)}) %copy-start) | copy-done | bytes 1179672
  39.7 0.0 copy-start.1
  39.7 1.2 %copy-done.1 = f32[2192,128]{1,0:T(8,128)S(1)} copy-done((f32[2192,128]{1,0:T(8,128)S(1)}, f32[2192,128]{1,0:T(8,128)}, u32[]{:S(2)}) %copy-start.1) | copy-done | bytes 1122328
  41.0 0.0 copy-start.2
  41.0 1.0 %copy-done.2 = f32[5,144,128]{2,1,0:T(8,128)S(1)} copy-done((f32[5,144,128]{2,1,0:T(8,128)S(1)}, f32[5,144,128]{2,1,0:T(8,128)}, u32[]{:S(2)}) %copy-start.2) | copy-done | bytes 368664
  42.0 3.2 %shard_map.87 = (f32[2192,128]{1,0:T(8,128)}, f32[2192,128]{1,0:T(8,128)}) custom-call(f32[2192,128]{1,0:T(8,128)S(1)} %copy-done.1, f32[16,144,128]{2,1,0:T(8,128)S(1)} %copy-done, f32[5,144,128]{2,1,0:T(8,128)S(1)} %copy-done.2, bf16[128,128]{1,0:T(8,128)(2,1)S(1)} %copy-done.3), custom_call_target="tpu_custom_call" | custom-call | tf_op jit(solution)/shard_map/pallas_call | solution.py:774
Async XLA Ops:
  0.6 37.8 %copy-start.3 = (bf16[128,128]{1,0:T(8,128)(2,1)S(1)}, bf16[128,128]{1,0:T(8,128)(2,1)}, u32[]{:S(2)}) copy-start(bf16[128,128]{1,0:T(8,128)(2,1)} %constant.8.clone.t_hbm) | copy-start | bytes 98308
  38.4 1.3 %copy-start = (f32[16,144,128]{2,1,0:T(8,128)S(1)}, f32[16,144,128]{2,1,0:T(8,128)}, u32[]{:S(2)}) copy-start(f32[16,144,128]{2,1,0:T(8,128)} %get-tuple-element.8.yz_hbm) | copy-start | bytes 3538948
  39.7 1.3 %copy-start.1 = (f32[2192,128]{1,0:T(8,128)S(1)}, f32[2192,128]{1,0:T(8,128)}, u32[]{:S(2)}) copy-start(f32[2192,128]{1,0:T(8,128)} %get-tuple-element.7.inc_hbm) | copy-start | bytes 3366916
  41.0 1.0 %copy-start.2 = (f32[5,144,128]{2,1,0:T(8,128)S(1)}, f32[5,144,128]{2,1,0:T(8,128)}, u32[]{:S(2)}) copy-start(f32[5,144,128]{2,1,0:T(8,128)} %get-tuple-element.9.pk_hbm) | copy-start | bytes 1105924

commit v7 on v5

--- a/solution.py
+++ b/solution.py
@@ -22,6 +22,8 @@
 NROWS = 42
 PACK = {2: (0, 1, -1, 64), 3: (66, 2, -1, 33), 4: (101, 3, -1, 17)}
 FOLD, WIDE = 16, 9
+CHUNKS = 2
+DIRECT = 11 - 2 * CHUNKS
 FOLD_LANES = LP // FOLD * WIDE
 LEVEL_OF = {}
 for _l in (1, 2, 3, 4):
@@ -256,6 +258,12 @@
     return jnp.dot(a, b, preferred_element_type=F32)
 
 
+def both(hi, lo, w):
+    if hi.shape[1] == 128:
+        return dot(jnp.concatenate([hi, lo], axis=1), jnp.concatenate([w, w], axis=0))
+    return dot(hi, w) + dot(lo, w)
+
+
 def kernel(x_hbm, vert_hbm, latf_hbm, lonf_hbm, cb_hbm, ext_hbm, inc_hbm, jump_hbm,
            x, vert, latf, lonf, cb, ext_c, inc, jump,
            xs, so, rw, lx, up, dn, p2, r_w, r_u, r_pw, r_pu, r_p2u, r_p2w,
@@ -300,7 +308,7 @@
     def mm(a, *key):
         hi, lo = split(a)
         w = const(key + ("hi",))
-        out = dot(hi, w) + dot(lo, w)
+        out = both(hi, lo, w)
         if key + ("lo",) in CWHERE:
             out = out + dot(hi, const(key + ("lo",)))
         return out
@@ -418,10 +426,10 @@
     low = lane < 64
     def vmul(ks, t):
         hi, lo = split(t)
-        both = jnp.concatenate([hi, lo], axis=1)
+        pair = jnp.concatenate([hi, lo], axis=1)
         outs = []
         for k in ks:
-            p = dot(vst[k][:, 0:LP], both)
+            p = dot(vst[k][:, 0:LP], pair)
             outs.append(p[0:LP, 0:128] + p[0:LP, 128:256] + p[LP:2 * LP, 0:128])
         return outs
 
@@ -429,10 +437,8 @@
         got = jnp.where(lane < BORDER[n], m_l[n], m_r[n])
         for k, js in users(n).items():
             hi, lo = split(vmul((k,), got)[0])
-            both = jnp.concatenate([hi, lo], axis=1)
             for c in range((len(js) + 1) // 2):
-                z = const(("Z", n, k, c, "hi"))
-                p = dot(both, jnp.concatenate([z, z], axis=0))
+                p = both(hi, lo, const(("Z", n, k, c, "hi")))
                 for h, j in enumerate(js[2 * c:2 * c + 2]):
                     at = j + 42 if k == 1 else j
                     bd[at] = bd[at] + p[:, 128 * h:128 * h + 128]
@@ -443,7 +449,7 @@
         else:
             h, l = split(operand(lo, hi))
             w = const(("W", 1, "hi"))[:, 128:256]
-            o1[lo:hi, :, 128:256] = (dot(h, w) + dot(l, w)).reshape(hi - lo, LP, 128)
+            o1[lo:hi, :, 128:256] = both(h, l, w).reshape(hi - lo, LP, 128)
 
     def bands1(js):
         for j in js:
@@ -499,30 +505,6 @@
     for i in range(1, 6):
         odd(i)
     level1(2, 13)
-    shift = [to_next(ys.at[pl.ds(2, 7)], prev.at[pl.ds(2, 7)])]
-    straight = remote(ys.at[pl.ds(9, 4)], prev.at[pl.ds(9, 4)], at_tm(1))
-    hops = []
-    for q in range(2):
-        mine, kept, there = ys.at[pl.ds(9 + 2 * q, 2)], way.at[pl.ds(2 * q, 2)], prev.at[pl.ds(9 + 2 * q, 2)]
-        hops.append((remote(mine, kept, at(3, across)), remote(kept, kept, at(0, lat)),
-                     remote(kept, there, at(2, across))))
-
-    @pl.when((tm == 0) | (tm == 2))
-    def _():
-        straight.start()
-
-    @pl.when(tm == 1)
-    def _():
-        for q in range(2):
-            hops[q][0].start()
-
-    def forward(window, hop):
-        @pl.when(tm == window)
-        def _():
-            for q in range(2):
-                hops[q][hop].wait_recv()
-                hops[q][hop + 1].start()
-
     for c in bulk:
         c.wait()
     x16 = lambda: mw * r_w[0]
@@ -541,6 +523,31 @@
 
     for c in packs:
         c.wait()
+
+    shift = [to_next(ys.at[pl.ds(2, DIRECT)], prev.at[pl.ds(2, DIRECT)])]
+    straight = remote(ys.at[pl.ds(2 + DIRECT, 2 * CHUNKS)], prev.at[pl.ds(2 + DIRECT, 2 * CHUNKS)], at_tm(1))
+    hops = []
+    for q in range(CHUNKS):
+        mine, kept, there = ys.at[pl.ds(2 + DIRECT + 2 * q, 2)], way.at[pl.ds(2 * q, 2)], prev.at[pl.ds(2 + DIRECT + 2 * q, 2)]
+        hops.append((remote(mine, kept, at(3, across)), remote(kept, kept, at(0, lat)),
+                     remote(kept, there, at(2, across))))
+
+    @pl.when((tm == 0) | (tm == 2))
+    def _():
+        straight.start()
+
+    @pl.when(tm == 1)
+    def _():
+        for q in range(CHUNKS):
+            hops[q][0].start()
+
+    def forward(window, hop):
+        @pl.when(tm == window)
+        def _():
+            for q in range(CHUNKS):
+                hops[q][hop].wait_recv()
+                hops[q][hop + 1].start()
+
     raw = lambda j: rw[j] if j < 19 else lx[j - 19, :, 0:128]
     for l in (2, 3, 4):
         m, a, d, b = MLAT[l], SROW[l - 1], DROW[l], SROW[l]
@@ -649,7 +656,7 @@
             tmsg[2 * i, :, 0:128] = rows[i]
             tmsg[2 * i + 1, :, 0:128] = 0.5 * (rows[i] + rows[i + 1])
         h, l = split(tmsg[0:16, :, 0:128].reshape(16 * LP, 128))
-        return (dot(h, w) + dot(l, w)).reshape(ROWS, LP, 128)
+        return both(h, l, w).reshape(ROWS, LP, 128)
 
     yz[...] = ys[...] + lifted(sm)
     for r in range(ROWS):
@@ -666,7 +673,7 @@
 
     @pl.when(tm == 2)
     def _():
-        for q in range(2):
+        for q in range(CHUNKS):
             hops[q][2].wait_recv()
 
     yz[...] = yz[...] - prev[...]
@@ -677,9 +684,9 @@
             part = pltpu.roll(part, 64, 1)
         end = pkp[4] if k == 0 else pltpu.roll(pkp[4], 128 - k, 1)
         sm[k] = jnp.where(lane == 64, end, part)
-    yz[...] = yz[...] - lifted(sm)
+    less = lifted(sm)
     for r in range(ROWS):
-        jump[pl.ds(r, LEV, stride=ROWS), :] = yz[r, 0:LEV, :]
+        jump[pl.ds(r, LEV, stride=ROWS), :] = yz[r, 0:LEV, :] - less[r, 0:LEV, :]
     out2 = pltpu.make_async_copy(jump, jump_hbm, load.at[7])
     out2.start()
     for c in shift:
@@ -688,7 +695,7 @@
     for window, hop in ((1, 0), (3, 1), (0, 2)):
         @pl.when(tm == window)
         def _(hop=hop):
-            for q in range(2):
+            for q in range(CHUNKS):
                 hops[q][hop].wait_send()
 
     out.wait()
@@ -712,7 +719,7 @@
         S((3,) + tile, F32), S((3,) + tile, F32), S((3,) + tile, F32),
         S((4, FOLD, 128), F32), S((4, FOLD, 128), F32), S((8, FOLD, 128), F32),
         S((52,) + tile, F32), S((9,) + tile, F32), S((5,) + tile, F32), S((5,) + tile, F32),
-        S((ROWS,) + tile, F32), S((ROWS,) + tile, F32), S((ROWS,) + tile, F32), S((4,) + tile, F32),
+        S((ROWS,) + tile, F32), S((ROWS,) + tile, F32), S((ROWS,) + tile, F32), S((2 * CHUNKS,) + tile, F32),
         pltpu.SemaphoreType.DMA((48,)), pltpu.SemaphoreType.DMA((48,)), pltpu.SemaphoreType.DMA((8,)),
     ]
     out = jax.ShapeDtypeStruct((LEV * ROWS, COLS), F32)

time: 41.2 us -> 39.9 us (0.968)
  the two profiles are of different devices: /device:TPU:6 before, /device:TPU:2 now
where the time goes in v7:
time: 39.9 us; the launch traced here: 39.3 us
  Pallas kernels  38.5 us (96%)
  between operations  0.8 us (2%)
    pallas_call x1, Pallas kernels, body(): pl.pallas_call(kernel, out_shape=(out, out), in_specs=[anywhere] * 6, out...  36 us
    pallas_call x1, Pallas kernels, body(): pl.pallas_call(settle, out_shape=(out, out), in_specs=[anywhere] * 2, out...  2.48 us

profile of v7, /device:TPU:2, one launch (start us, length us, event | category | flops | bytes accessed | tf_op | source)
XLA Modules:
  0.0 39.3 jit_solution(15728378338348301792)
XLA Ops:
  0.6 36.0 %shard_map.77 = (f32[2192,128]{1,0:T(8,128)}, f32[2192,128]{1,0:T(8,128)}) custom-call(f32[2192,128]{1,0:T(8,128)} %bitcast.3, f32[13,137,137]{2,1,0:T(8,128)} %vert_hbm.1, f32[8,8]{1,0:T(8,128)} %latf_hbm.1, f32[32,32]{1,0:T(8,128)} %lonf_hbm.1, bf16[8704,256]{1,0:T(8,128)(2,1)} %constant.4.clone.cb_hbm, f32[48,128]{1,0:T(8,128)} %constant.5.clone.ext_hbm), custom_call_target="tpu_custom_call" | custom-call | tf_op jit(solution)/shard_map/pallas_call | solution.py:726
  36.6 2.5 %shard_map.78 = (f32[2192,128]{1,0:T(8,128)}, f32[2192,128]{1,0:T(8,128)}) custom-call(f32[2192,128]{1,0:T(8,128)} %get-tuple-element.6.a, f32[2192,128]{1,0:T(8,128)} %get-tuple-element.7.b), custom_call_target="tpu_custom_call" | custom-call | tf_op jit(solution)/shard_map/pallas_call | solution.py:752

commit v8 on v7

--- a/solution.py
+++ b/solution.py
@@ -295,7 +295,7 @@
         pl.semaphore_signal(barrier, inc=1, device_id=p, device_id_type=MESH)
 
     loads = {}
-    for n, (name, src, dst) in enumerate((("x", x_hbm, x), ("cb", cb_hbm, cb), ("ext", ext_hbm, ext_c),
+    for n, (name, src, dst) in enumerate((("x", x_hbm, x.at[pl.ds(0, LEV * ROWS)]), ("cb", cb_hbm, cb), ("ext", ext_hbm, ext_c),
                                           ("lonf", lonf_hbm, lonf), ("latf", latf_hbm, latf),
                                           ("vert", vert_hbm, vert))):
         loads[name] = pltpu.make_async_copy(src, dst, load.at[n])
@@ -661,7 +661,7 @@
     yz[...] = ys[...] + lifted(sm)
     for r in range(ROWS):
         inc[pl.ds(r, LEV, stride=ROWS), :] = yz[r, 0:LEV, :]
-    out = pltpu.make_async_copy(inc, inc_hbm, load.at[6])
+    out = pltpu.make_async_copy(inc.at[pl.ds(0, LEV * ROWS)], inc_hbm, load.at[6])
     out.start()
 
     def land(cs):
@@ -687,7 +687,7 @@
     less = lifted(sm)
     for r in range(ROWS):
         jump[pl.ds(r, LEV, stride=ROWS), :] = yz[r, 0:LEV, :] - less[r, 0:LEV, :]
-    out2 = pltpu.make_async_copy(jump, jump_hbm, load.at[7])
+    out2 = pltpu.make_async_copy(jump.at[pl.ds(0, LEV * ROWS)], jump_hbm, load.at[7])
     out2.start()
     for c in shift:
         pl.when(tm < 3)(c.wait_send)
@@ -707,10 +707,10 @@
     tile = (LP, 128)
     anywhere = pl.BlockSpec(memory_space=pl.ANY)
     S = pltpu.VMEM
-    flat = (LEV * ROWS, COLS)
+    flat, roomy = (LEV * ROWS, COLS), (LP * ROWS, COLS)
     scratch = [
-        S(flat, F32), S((BANDS, LEV, LEV), F32), S((8, 8), F32), S((32, 32), F32), S(CB.shape, BF), S(EXT.shape, F32),
-        S(flat, F32), S(flat, F32),
+        S(roomy, F32), S((BANDS, LEV, LEV), F32), S((8, 8), F32), S((32, 32), F32), S(CB.shape, BF), S(EXT.shape, F32),
+        S(roomy, F32), S(roomy, F32),
         S((ROWS,) + tile, F32), S((39,) + tile, F32), S((19,) + tile, F32), S((23, LP, 256), F32),
         S((3,) + tile, F32), S((2,) + tile, F32), S((2,) + tile, F32),
         S((2,) + tile, F32), S(tile, F32), S(tile, F32), S(tile, F32), S(tile, F32), S(tile, F32),

time: 39.9 us -> 39.9 us (level)
  no operation moved by 1% of the time
where the time goes in v8:
time: 39.9 us; the launch traced here: 39.3 us
  Pallas kernels  38.5 us (96%)
  between operations  0.8 us (2%)
    pallas_call x1, Pallas kernels, body(): pl.pallas_call(kernel, out_shape=(out, out), in_specs=[anywhere] * 6, out...  36 us
    pallas_call x1, Pallas kernels, body(): pl.pallas_call(settle, out_shape=(out, out), in_specs=[anywhere] * 2, out...  2.48 us

profile of v8, /device:TPU:2, one launch (start us, length us, event | category | flops | bytes accessed | tf_op | source)
XLA Modules:
  0.0 39.3 jit_solution(11879939983314872077)
XLA Ops:
  0.6 36.0 %shard_map.77 = (f32[2192,128]{1,0:T(8,128)}, f32[2192,128]{1,0:T(8,128)}) custom-call(f32[2192,128]{1,0:T(8,128)} %bitcast.3, f32[13,137,137]{2,1,0:T(8,128)} %vert_hbm.1, f32[8,8]{1,0:T(8,128)} %latf_hbm.1, f32[32,32]{1,0:T(8,128)} %lonf_hbm.1, bf16[8704,256]{1,0:T(8,128)(2,1)} %constant.4.clone.cb_hbm, f32[48,128]{1,0:T(8,128)} %constant.5.clone.ext_hbm), custom_call_target="tpu_custom_call" | custom-call | tf_op jit(solution)/shard_map/pallas_call | solution.py:726
  36.6 2.5 %shard_map.78 = (f32[2192,128]{1,0:T(8,128)}, f32[2192,128]{1,0:T(8,128)}) custom-call(f32[2192,128]{1,0:T(8,128)} %get-tuple-element.6.a, f32[2192,128]{1,0:T(8,128)} %get-tuple-element.7.b), custom_call_target="tpu_custom_call" | custom-call | tf_op jit(solution)/shard_map/pallas_call | solution.py:752
